TPU v7x, 512 devices: a whole 4x4x16 slice. The times are simulated.
512 devices in a mesh: segment: 8 (over y, core), rows: 16 (over z), dp: 4 (over x).
Axes of the slice: x: 4, y: 4, z: 16, core: 2. Of those that a mesh axis runs over, the one named last changes fastest.
Arguments:
- clips: bfloat16 [4, 4, 4, 128, 8, 128], P(None, 'dp', None, 'rows'), may hold values from -80 to 80
- lengths: int32 [4, 4], P(None, 'dp'), may hold values from 1 to 4, as said below
- conv_weight: bfloat16 [8, 3456, 128], P('segment'), may hold values from -0.109375 to 0.109375
- norm_gain: float32 [8, 128], P('segment'), may hold values from 0.5 to 2
- norm_shift: float32 [8, 128], P('segment'), may hold values from -1 to 1
- conv_bias: float32 [8, 128], P('segment'), may hold values from -3 to 3
- cotangent: bfloat16 [8, 4, 4, 4, 128, 8, 128], P('segment', None, 'dp', None, 'rows'), may hold values from -6 to 6
Outputs:
- stash: bfloat16 [8, 4, 4, 4, 128, 8, 128], P('segment', None, 'dp', None, 'rows')
- weight_grad: float32 [8, 3456, 128], P('segment')
Inputs may be any that keep to these rules, and one draw needn't show every extreme that they name: lengths[m, clip] real frames lead each clip; the frames after them are padding; some clip has all 4 frames.
All inputs are finite; a program needn't handle non-finite values.
Results may differ from a plain program's by a relative error of at most 0.009.
Values may be sent and summed in bfloat16 or wider, within the bound.
A program may use at most 64 MiB of HBM per device.

v0:
```python
import math

import jax
import jax.numpy as jnp
from jax import lax
from jax.sharding import PartitionSpec as P

GROUPS = 32


eps = 1e-06


def extended_2(cells, sides, width):
    for axis, dim in sides:
        count = lax.axis_size(axis)
        ends = count - 1
        head = lax.slice_in_dim(cells, 0, width, axis=dim)
        tail = lax.slice_in_dim(cells, cells.shape[dim] - width, cells.shape[dim], axis=dim)
        cells = jnp.concatenate(
            [
                lax.ppermute(tail, axis, [(i, (i + 1) % count) for i in range(ends)]),
                cells,
                lax.ppermute(head, axis, [((i + 1) % count, i) for i in range(ends)]),
            ],
            axis=dim,
        )
    return cells


def passed_along(block, axis, distance):
    devices = range(lax.axis_size(axis))
    route = [(i - distance, i) for i in devices if i - distance in devices]
    return lax.ppermute(block, axis, route)


def statistics(values, frame_mask, length, height):
    clip_count, frames, rows_here, cols, chans = values.shape
    sub = chans // GROUPS
    grouped = values.reshape(clip_count, frames, rows_here, cols, GROUPS, sub)
    mask_six = frame_mask[:, :, :, :, :, None]
    count = (length * (height * cols * sub)).astype(jnp.float32)[:, None]
    total = lax.psum(jnp.sum(grouped * mask_six, axis=(1, 2, 3, 5)), "rows")
    mean = total / count
    centered = grouped - mean[:, None, None, None, :, None]
    spread = lax.psum(jnp.sum(centered * centered * mask_six, axis=(1, 2, 3, 5)), "rows")
    var = spread / count
    rstd = lax.rsqrt(var + eps)
    mean_chan = jnp.repeat(mean, sub, axis=-1)[:, None, None, None, :]
    rstd_chan = jnp.repeat(rstd, sub, axis=-1)[:, None, None, None, :]
    return (mean_chan, rstd_chan)


def block(current, length, weight, gain, shift, bias, height):
    clip_count, frames, rows_here, cols, chans = current.shape
    values = current.astype(jnp.float32)
    frame_mask = (jnp.arange(frames)[None, :] < length[:, None]).astype(jnp.float32)[
        :, :, None, None, None
    ]
    mean_chan, rstd_chan = statistics(values, frame_mask, length, height)
    hidden = jax.nn.silu((values - mean_chan) * rstd_chan * gain + shift).astype(jnp.bfloat16)
    extended = extended_2(hidden, (("rows", 2),), 1)
    padded = jnp.pad(extended, ((0, 0), (0, 0), (0, 0), (1, 1), (0, 0)))
    padded = jnp.concatenate([padded[:, :1], padded[:, :1], padded], axis=1)
    pieces = []
    for tap_t in range(3):
        for tap_h in range(3):
            for tap_w in range(3):
                pieces.append(
                    padded[
                        :,
                        tap_t : tap_t + frames,
                        tap_h : tap_h + rows_here,
                        tap_w : tap_w + cols,
                        :,
                    ]
                )
    patches = jnp.concatenate(pieces, axis=-1).reshape(-1, 27 * chans)
    conv = jnp.dot(patches, weight, preferred_element_type=jnp.float32).reshape(values.shape)
    result = ((values + conv + bias) * frame_mask).astype(jnp.bfloat16)
    return (result, patches, frame_mask.astype(jnp.bfloat16))


def per_device(clips, lengths, conv_weight, norm_gain, norm_shift, conv_bias, cotangent):
    segments = lax.axis_size("segment")
    segment_id = lax.axis_index("segment")
    micro = clips.shape[0]
    frames = clips.shape[2]
    cols = clips.shape[4]
    chans = clips.shape[5]
    height = clips.shape[3] * lax.axis_size("rows")
    weight = conv_weight[0]
    gain = norm_gain[0]
    shift = norm_shift[0]
    bias = conv_bias[0]
    cot_all = cotangent[0]
    total_cells = micro * clips.shape[1] * lax.axis_size("dp") * frames * height * cols
    factor = 1.0 / math.sqrt(total_cells)

    def tick(step, carry):
        arrived, stash, grads = carry
        which = step - segment_id
        valid = (which >= 0) & (which < micro)
        slot = jnp.clip(which, 0, micro - 1)
        fresh = lax.dynamic_index_in_dim(
            clips, jnp.clip(step, 0, micro - 1).astype(jnp.int32), 0, keepdims=False
        )
        current = jnp.where(segment_id == 0, fresh, arrived)
        length = lax.dynamic_index_in_dim(lengths, slot, 0, keepdims=False)
        result, patches, mask_five = block(current, length, weight, gain, shift, bias, height)
        cot_now = lax.dynamic_index_in_dim(cot_all, slot, 0, keepdims=False)
        masked = (cot_now * mask_five).reshape(-1, chans)
        term = lax.dot_general(
            patches, masked, (((0,), (0,)), ((), ())), preferred_element_type=jnp.float32
        )
        grads = grads + jnp.where(valid, term, 0.0)
        previous = lax.dynamic_index_in_dim(stash, slot, 0, keepdims=False)
        stash = lax.dynamic_update_index_in_dim(stash, jnp.where(valid, result, previous), slot, 0)
        arrived = passed_along(result, "segment", 1)
        return (arrived, stash, grads)

    start = (
        jnp.zeros(clips.shape[1:], jnp.bfloat16),
        jnp.zeros(clips.shape, jnp.bfloat16),
        jnp.zeros((27 * chans, chans), jnp.float32),
    )
    arrived, stash, grads = lax.fori_loop(0, micro + segments - 1, tick, start)
    grads = lax.psum(grads, ("rows", "dp")) * factor
    return (stash[None], grads[None])


def solution(mesh):
    in_specs = (
        P(None, "dp", None, "rows", None, None),
        P(None, "dp"),
        P("segment", None, None),
        P("segment", None),
        P("segment", None),
        P("segment", None),
        P("segment", None, "dp", None, "rows", None, None),
    )
    out_specs = (P("segment", None, "dp", None, "rows", None, None), P("segment", None, None))
    return jax.shard_map(
        per_device, mesh=mesh, in_specs=in_specs, out_specs=out_specs, check_vma=False
    )
```

profile of v0, /device:TPU:25, one launch (start us, length us, event | category | flops | bytes accessed | tf_op | source)
XLA Modules:
  0.0 1151.4 jit_solution(13718055022507466365)
XLA Ops:
  7.3 864.9 %while.20 = (s32[]{:T(128)}, bf16[1,4,8,8,128]{4,3,2,1,0:T(8,128)(2,1)S(1)}, bf16[4,1,4,8,8,128]{5,4,3,2,1,0:T(8,128)(2,1)S(1)}, f32[3456,128]{1,0:T(8,128)S(1)}...) while((s32[]{:T(128)}, ...), condition=%wide.region_7.8_spmd.clone, body=%wide.region_0.7_spmd.clone.sunk | while | flops 457701504 | bytes 18060908 | solution.py:127
  10.4 29.5 %psum.40 = f32[1,32]{1,0:T(1,128)S(1)} all-reduce(f32[1,32]{1,0:T(1,128)S(1)} %bitcast.110), channel_id=1, replica_groups=mesh['segment'=8,'rows'=16,'dp'=4] {'rows'}, use_global_device_ids=true, to_apply=%region_3.3 | all-reduce | flops 32 | bytes 256 | tf_op jit(solution)/shard_map/while/body/eval_jaxpr/psum | solution.py:43
  41.1 20.1 %psum.41 = f32[1,32]{1,0:T(1,128)S(1)} all-reduce(f32[1,32]{1,0:T(1,128)S(1)} %bitcast.109), channel_id=1, replica_groups=mesh['segment'=8,'rows'=16,'dp'=4] {'rows'}, use_global_device_ids=true, to_apply=%region_6.6 | all-reduce | flops 32 | bytes 256 | tf_op jit(solution)/shard_map/while/body/eval_jaxpr/psum | solution.py:46
  91.9 23.3 %psum.40 = f32[1,32]{1,0:T(1,128)S(1)} all-reduce(f32[1,32]{1,0:T(1,128)S(1)} %bitcast.110), channel_id=1, replica_groups=mesh['segment'=8,'rows'=16,'dp'=4] {'rows'}, use_global_device_ids=true, to_apply=%region_3.3 | all-reduce | flops 32 | bytes 256 | tf_op jit(solution)/shard_map/while/body/eval_jaxpr/psum | solution.py:43
  116.3 21.8 %psum.41 = f32[1,32]{1,0:T(1,128)S(1)} all-reduce(f32[1,32]{1,0:T(1,128)S(1)} %bitcast.109), channel_id=1, replica_groups=mesh['segment'=8,'rows'=16,'dp'=4] {'rows'}, use_global_device_ids=true, to_apply=%region_6.6 | all-reduce | flops 32 | bytes 256 | tf_op jit(solution)/shard_map/while/body/eval_jaxpr/psum | solution.py:46
  151.1 17.6 %collective-permute-done.2 = bf16[1,4,8,8,128]{4,3,2,1,0:T(8,128)(2,1)S(1)} collective-permute-done((bf16[1,4,8,8,128]{4,3,2,1,0:T(8,128)(2,1)S(1)}, bf16[1,4,8,8,128]{4,3,2,1,0:T(8,128)(2,1)S(1)}, u32[]{:S(2)}, u32[]{:S(2)}) %collective-permute-start.2) | collective-permute-done | bytes 65568 | tf_op jit(solution)/shard_map/while/body/eval_jaxpr/ppermute | solution.py:34
  171.7 22.1 %psum.40 = f32[1,32]{1,0:T(1,128)S(1)} all-reduce(f32[1,32]{1,0:T(1,128)S(1)} %bitcast.110), channel_id=1, replica_groups=mesh['segment'=8,'rows'=16,'dp'=4] {'rows'}, use_global_device_ids=true, to_apply=%region_3.3 | all-reduce | flops 32 | bytes 256 | tf_op jit(solution)/shard_map/while/body/eval_jaxpr/psum | solution.py:43
  195.0 21.5 %psum.41 = f32[1,32]{1,0:T(1,128)S(1)} all-reduce(f32[1,32]{1,0:T(1,128)S(1)} %bitcast.109), channel_id=1, replica_groups=mesh['segment'=8,'rows'=16,'dp'=4] {'rows'}, use_global_device_ids=true, to_apply=%region_6.6 | all-reduce | flops 32 | bytes 256 | tf_op jit(solution)/shard_map/while/body/eval_jaxpr/psum | solution.py:46
  249.5 22.1 %psum.40 = f32[1,32]{1,0:T(1,128)S(1)} all-reduce(f32[1,32]{1,0:T(1,128)S(1)} %bitcast.110), channel_id=1, replica_groups=mesh['segment'=8,'rows'=16,'dp'=4] {'rows'}, use_global_device_ids=true, to_apply=%region_3.3 | all-reduce | flops 32 | bytes 256 | tf_op jit(solution)/shard_map/while/body/eval_jaxpr/psum | solution.py:43
  272.8 21.8 %psum.41 = f32[1,32]{1,0:T(1,128)S(1)} all-reduce(f32[1,32]{1,0:T(1,128)S(1)} %bitcast.109), channel_id=1, replica_groups=mesh['segment'=8,'rows'=16,'dp'=4] {'rows'}, use_global_device_ids=true, to_apply=%region_6.6 | all-reduce | flops 32 | bytes 256 | tf_op jit(solution)/shard_map/while/body/eval_jaxpr/psum | solution.py:46
  307.5 17.6 %collective-permute-done.2 = bf16[1,4,8,8,128]{4,3,2,1,0:T(8,128)(2,1)S(1)} collective-permute-done((bf16[1,4,8,8,128]{4,3,2,1,0:T(8,128)(2,1)S(1)}, bf16[1,4,8,8,128]{4,3,2,1,0:T(8,128)(2,1)S(1)}, u32[]{:S(2)}, u32[]{:S(2)}) %collective-permute-start.2) | collective-permute-done | bytes 65568 | tf_op jit(solution)/shard_map/while/body/eval_jaxpr/ppermute | solution.py:34
  328.1 22.1 %psum.40 = f32[1,32]{1,0:T(1,128)S(1)} all-reduce(f32[1,32]{1,0:T(1,128)S(1)} %bitcast.110), channel_id=1, replica_groups=mesh['segment'=8,'rows'=16,'dp'=4] {'rows'}, use_global_device_ids=true, to_apply=%region_3.3 | all-reduce | flops 32 | bytes 256 | tf_op jit(solution)/shard_map/while/body/eval_jaxpr/psum | solution.py:43
  351.4 21.5 %psum.41 = f32[1,32]{1,0:T(1,128)S(1)} all-reduce(f32[1,32]{1,0:T(1,128)S(1)} %bitcast.109), channel_id=1, replica_groups=mesh['segment'=8,'rows'=16,'dp'=4] {'rows'}, use_global_device_ids=true, to_apply=%region_6.6 | all-reduce | flops 32 | bytes 256 | tf_op jit(solution)/shard_map/while/body/eval_jaxpr/psum | solution.py:46
  385.8 17.1 %collective-permute-done.2 = bf16[1,4,8,8,128]{4,3,2,1,0:T(8,128)(2,1)S(1)} collective-permute-done((bf16[1,4,8,8,128]{4,3,2,1,0:T(8,128)(2,1)S(1)}, bf16[1,4,8,8,128]{4,3,2,1,0:T(8,128)(2,1)S(1)}, u32[]{:S(2)}, u32[]{:S(2)}) %collective-permute-start.2) | collective-permute-done | bytes 65568 | tf_op jit(solution)/shard_map/while/body/eval_jaxpr/ppermute | solution.py:34
  406.0 22.1 %psum.40 = f32[1,32]{1,0:T(1,128)S(1)} all-reduce(f32[1,32]{1,0:T(1,128)S(1)} %bitcast.110), channel_id=1, replica_groups=mesh['segment'=8,'rows'=16,'dp'=4] {'rows'}, use_global_device_ids=true, to_apply=%region_3.3 | all-reduce | flops 32 | bytes 256 | tf_op jit(solution)/shard_map/while/body/eval_jaxpr/psum | solution.py:43
  429.2 21.8 %psum.41 = f32[1,32]{1,0:T(1,128)S(1)} all-reduce(f32[1,32]{1,0:T(1,128)S(1)} %bitcast.109), channel_id=1, replica_groups=mesh['segment'=8,'rows'=16,'dp'=4] {'rows'}, use_global_device_ids=true, to_apply=%region_6.6 | all-reduce | flops 32 | bytes 256 | tf_op jit(solution)/shard_map/while/body/eval_jaxpr/psum | solution.py:46
  463.9 17.6 %collective-permute-done.2 = bf16[1,4,8,8,128]{4,3,2,1,0:T(8,128)(2,1)S(1)} collective-permute-done((bf16[1,4,8,8,128]{4,3,2,1,0:T(8,128)(2,1)S(1)}, bf16[1,4,8,8,128]{4,3,2,1,0:T(8,128)(2,1)S(1)}, u32[]{:S(2)}, u32[]{:S(2)}) %collective-permute-start.2) | collective-permute-done | bytes 65568 | tf_op jit(solution)/shard_map/while/body/eval_jaxpr/ppermute | solution.py:34
  484.6 22.1 %psum.40 = f32[1,32]{1,0:T(1,128)S(1)} all-reduce(f32[1,32]{1,0:T(1,128)S(1)} %bitcast.110), channel_id=1, replica_groups=mesh['segment'=8,'rows'=16,'dp'=4] {'rows'}, use_global_device_ids=true, to_apply=%region_3.3 | all-reduce | flops 32 | bytes 256 | tf_op jit(solution)/shard_map/while/body/eval_jaxpr/psum | solution.py:43
  507.8 21.5 %psum.41 = f32[1,32]{1,0:T(1,128)S(1)} all-reduce(f32[1,32]{1,0:T(1,128)S(1)} %bitcast.109), channel_id=1, replica_groups=mesh['segment'=8,'rows'=16,'dp'=4] {'rows'}, use_global_device_ids=true, to_apply=%region_6.6 | all-reduce | flops 32 | bytes 256 | tf_op jit(solution)/shard_map/while/body/eval_jaxpr/psum | solution.py:46
  562.4 22.1 %psum.40 = f32[1,32]{1,0:T(1,128)S(1)} all-reduce(f32[1,32]{1,0:T(1,128)S(1)} %bitcast.110), channel_id=1, replica_groups=mesh['segment'=8,'rows'=16,'dp'=4] {'rows'}, use_global_device_ids=true, to_apply=%region_3.3 | all-reduce | flops 32 | bytes 256 | tf_op jit(solution)/shard_map/while/body/eval_jaxpr/psum | solution.py:43
  585.6 21.8 %psum.41 = f32[1,32]{1,0:T(1,128)S(1)} all-reduce(f32[1,32]{1,0:T(1,128)S(1)} %bitcast.109), channel_id=1, replica_groups=mesh['segment'=8,'rows'=16,'dp'=4] {'rows'}, use_global_device_ids=true, to_apply=%region_6.6 | all-reduce | flops 32 | bytes 256 | tf_op jit(solution)/shard_map/while/body/eval_jaxpr/psum | solution.py:46
  620.4 17.6 %collective-permute-done.2 = bf16[1,4,8,8,128]{4,3,2,1,0:T(8,128)(2,1)S(1)} collective-permute-done((bf16[1,4,8,8,128]{4,3,2,1,0:T(8,128)(2,1)S(1)}, bf16[1,4,8,8,128]{4,3,2,1,0:T(8,128)(2,1)S(1)}, u32[]{:S(2)}, u32[]{:S(2)}) %collective-permute-start.2) | collective-permute-done | bytes 65568 | tf_op jit(solution)/shard_map/while/body/eval_jaxpr/ppermute | solution.py:34
  641.0 22.1 %psum.40 = f32[1,32]{1,0:T(1,128)S(1)} all-reduce(f32[1,32]{1,0:T(1,128)S(1)} %bitcast.110), channel_id=1, replica_groups=mesh['segment'=8,'rows'=16,'dp'=4] {'rows'}, use_global_device_ids=true, to_apply=%region_3.3 | all-reduce | flops 32 | bytes 256 | tf_op jit(solution)/shard_map/while/body/eval_jaxpr/psum | solution.py:43
  664.2 21.5 %psum.41 = f32[1,32]{1,0:T(1,128)S(1)} all-reduce(f32[1,32]{1,0:T(1,128)S(1)} %bitcast.109), channel_id=1, replica_groups=mesh['segment'=8,'rows'=16,'dp'=4] {'rows'}, use_global_device_ids=true, to_apply=%region_6.6 | all-reduce | flops 32 | bytes 256 | tf_op jit(solution)/shard_map/while/body/eval_jaxpr/psum | solution.py:46
  698.7 17.1 %collective-permute-done.2 = bf16[1,4,8,8,128]{4,3,2,1,0:T(8,128)(2,1)S(1)} collective-permute-done((bf16[1,4,8,8,128]{4,3,2,1,0:T(8,128)(2,1)S(1)}, bf16[1,4,8,8,128]{4,3,2,1,0:T(8,128)(2,1)S(1)}, u32[]{:S(2)}, u32[]{:S(2)}) %collective-permute-start.2) | collective-permute-done | bytes 65568 | tf_op jit(solution)/shard_map/while/body/eval_jaxpr/ppermute | solution.py:34
  718.8 22.1 %psum.40 = f32[1,32]{1,0:T(1,128)S(1)} all-reduce(f32[1,32]{1,0:T(1,128)S(1)} %bitcast.110), channel_id=1, replica_groups=mesh['segment'=8,'rows'=16,'dp'=4] {'rows'}, use_global_device_ids=true, to_apply=%region_3.3 | all-reduce | flops 32 | bytes 256 | tf_op jit(solution)/shard_map/while/body/eval_jaxpr/psum | solution.py:43
  742.1 21.8 %psum.41 = f32[1,32]{1,0:T(1,128)S(1)} all-reduce(f32[1,32]{1,0:T(1,128)S(1)} %bitcast.109), channel_id=1, replica_groups=mesh['segment'=8,'rows'=16,'dp'=4] {'rows'}, use_global_device_ids=true, to_apply=%region_6.6 | all-reduce | flops 32 | bytes 256 | tf_op jit(solution)/shard_map/while/body/eval_jaxpr/psum | solution.py:46
  776.8 17.6 %collective-permute-done.2 = bf16[1,4,8,8,128]{4,3,2,1,0:T(8,128)(2,1)S(1)} collective-permute-done((bf16[1,4,8,8,128]{4,3,2,1,0:T(8,128)(2,1)S(1)}, bf16[1,4,8,8,128]{4,3,2,1,0:T(8,128)(2,1)S(1)}, u32[]{:S(2)}, u32[]{:S(2)}) %collective-permute-start.2) | collective-permute-done | bytes 65568 | tf_op jit(solution)/shard_map/while/body/eval_jaxpr/ppermute | solution.py:34
  797.4 22.1 %psum.40 = f32[1,32]{1,0:T(1,128)S(1)} all-reduce(f32[1,32]{1,0:T(1,128)S(1)} %bitcast.110), channel_id=1, replica_groups=mesh['segment'=8,'rows'=16,'dp'=4] {'rows'}, use_global_device_ids=true, to_apply=%region_3.3 | all-reduce | flops 32 | bytes 256 | tf_op jit(solution)/shard_map/while/body/eval_jaxpr/psum | solution.py:43
  820.7 21.5 %psum.41 = f32[1,32]{1,0:T(1,128)S(1)} all-reduce(f32[1,32]{1,0:T(1,128)S(1)} %bitcast.109), channel_id=1, replica_groups=mesh['segment'=8,'rows'=16,'dp'=4] {'rows'}, use_global_device_ids=true, to_apply=%region_6.6 | all-reduce | flops 32 | bytes 256 | tf_op jit(solution)/shard_map/while/body/eval_jaxpr/psum | solution.py:46
  855.1 17.1 %collective-permute-done.2 = bf16[1,4,8,8,128]{4,3,2,1,0:T(8,128)(2,1)S(1)} collective-permute-done((bf16[1,4,8,8,128]{4,3,2,1,0:T(8,128)(2,1)S(1)}, bf16[1,4,8,8,128]{4,3,2,1,0:T(8,128)(2,1)S(1)}, u32[]{:S(2)}, u32[]{:S(2)}) %collective-permute-start.2) | collective-permute-done | bytes 65568 | tf_op jit(solution)/shard_map/while/body/eval_jaxpr/ppermute | solution.py:34
  873.5 268.3 %all-reduce.3.cloned.1.call-done = f32[3456,128]{1,0:T(8,128)} async-done(((f32[3456,128]{1,0:T(8,128)}), f32[3456,128]{1,0:T(8,128)}) %all-reduce.3.cloned.1.call-update) | async-done | bytes 1769488 | tf_op jit(solution)/shard_map/psum | solution.py:128
  (706 shorter events, 231.2 us)
Async XLA Ops:
  7.2 1134.6 %all-reduce.3.cloned.1.call-start = ((), (), s32[]{:S(2)}) async-start(), calls=%async_computation | async-start | bytes 3538944 | tf_op jit(solution)/shard_map/psum | solution.py:128
  62.1 5.9 collective-permute-start
  63.4 4.8 collective-permute-start.1
  70.5 18.4 %collective-permute-start.2 = (bf16[1,4,8,8,128]{4,3,2,1,0:T(8,128)(2,1)S(1)}, bf16[1,4,8,8,128]{4,3,2,1,0:T(8,128)(2,1)S(1)}, u32[]{:S(2)}, u32[]{:S(2)}) collective-permute-start(bf16[1,4,8,8,128]{4,3,2,1,0:T(8,128)(2,1)S(1)} %get-tuple-element.466), channel_id=1, source_target_pairs={{0,64},{64,128},{128,192},{192,256},{256,320},{320,384},{384,448},... | collective-permute-start | bytes 196616 | tf_op jit(solution)/shard_map/while/body/eval_jaxpr/ppermute | solution.py:34
  139.1 5.9 collective-permute-start
  140.4 4.8 collective-permute-start.1
  147.5 21.2 %collective-permute-start.2 = (bf16[1,4,8,8,128]{4,3,2,1,0:T(8,128)(2,1)S(1)}, bf16[1,4,8,8,128]{4,3,2,1,0:T(8,128)(2,1)S(1)}, u32[]{:S(2)}, u32[]{:S(2)}) collective-permute-start(bf16[1,4,8,8,128]{4,3,2,1,0:T(8,128)(2,1)S(1)} %get-tuple-element.466), channel_id=1, source_target_pairs={{0,64},{64,128},{128,192},{192,256},{256,320},{320,384},{384,448},... | collective-permute-start | bytes 196616 | tf_op jit(solution)/shard_map/while/body/eval_jaxpr/ppermute | solution.py:34
  217.4 5.9 collective-permute-start
  218.7 4.8 collective-permute-start.1
  225.8 20.7 %collective-permute-start.2 = (bf16[1,4,8,8,128]{4,3,2,1,0:T(8,128)(2,1)S(1)}, bf16[1,4,8,8,128]{4,3,2,1,0:T(8,128)(2,1)S(1)}, u32[]{:S(2)}, u32[]{:S(2)}) collective-permute-start(bf16[1,4,8,8,128]{4,3,2,1,0:T(8,128)(2,1)S(1)} %get-tuple-element.466), channel_id=1, source_target_pairs={{0,64},{64,128},{128,192},{192,256},{256,320},{320,384},{384,448},... | collective-permute-start | bytes 196616 | tf_op jit(solution)/shard_map/while/body/eval_jaxpr/ppermute | solution.py:34
  295.5 5.9 collective-permute-start
  296.8 4.8 collective-permute-start.1
  303.9 21.2 %collective-permute-start.2 = (bf16[1,4,8,8,128]{4,3,2,1,0:T(8,128)(2,1)S(1)}, bf16[1,4,8,8,128]{4,3,2,1,0:T(8,128)(2,1)S(1)}, u32[]{:S(2)}, u32[]{:S(2)}) collective-permute-start(bf16[1,4,8,8,128]{4,3,2,1,0:T(8,128)(2,1)S(1)} %get-tuple-element.466), channel_id=1, source_target_pairs={{0,64},{64,128},{128,192},{192,256},{256,320},{320,384},{384,448},... | collective-permute-start | bytes 196616 | tf_op jit(solution)/shard_map/while/body/eval_jaxpr/ppermute | solution.py:34
  373.9 5.9 collective-permute-start
  375.2 4.8 collective-permute-start.1
  382.3 20.7 %collective-permute-start.2 = (bf16[1,4,8,8,128]{4,3,2,1,0:T(8,128)(2,1)S(1)}, bf16[1,4,8,8,128]{4,3,2,1,0:T(8,128)(2,1)S(1)}, u32[]{:S(2)}, u32[]{:S(2)}) collective-permute-start(bf16[1,4,8,8,128]{4,3,2,1,0:T(8,128)(2,1)S(1)} %get-tuple-element.466), channel_id=1, source_target_pairs={{0,64},{64,128},{128,192},{192,256},{256,320},{320,384},{384,448},... | collective-permute-start | bytes 196616 | tf_op jit(solution)/shard_map/while/body/eval_jaxpr/ppermute | solution.py:34
  452.0 5.9 collective-permute-start
  453.3 4.8 collective-permute-start.1
  460.4 21.2 %collective-permute-start.2 = (bf16[1,4,8,8,128]{4,3,2,1,0:T(8,128)(2,1)S(1)}, bf16[1,4,8,8,128]{4,3,2,1,0:T(8,128)(2,1)S(1)}, u32[]{:S(2)}, u32[]{:S(2)}) collective-permute-start(bf16[1,4,8,8,128]{4,3,2,1,0:T(8,128)(2,1)S(1)} %get-tuple-element.466), channel_id=1, source_target_pairs={{0,64},{64,128},{128,192},{192,256},{256,320},{320,384},{384,448},... | collective-permute-start | bytes 196616 | tf_op jit(solution)/shard_map/while/body/eval_jaxpr/ppermute | solution.py:34
  530.3 5.9 collective-permute-start
  531.6 4.8 collective-permute-start.1
  538.7 20.7 %collective-permute-start.2 = (bf16[1,4,8,8,128]{4,3,2,1,0:T(8,128)(2,1)S(1)}, bf16[1,4,8,8,128]{4,3,2,1,0:T(8,128)(2,1)S(1)}, u32[]{:S(2)}, u32[]{:S(2)}) collective-permute-start(bf16[1,4,8,8,128]{4,3,2,1,0:T(8,128)(2,1)S(1)} %get-tuple-element.466), channel_id=1, source_target_pairs={{0,64},{64,128},{128,192},{192,256},{256,320},{320,384},{384,448},... | collective-permute-start | bytes 196616 | tf_op jit(solution)/shard_map/while/body/eval_jaxpr/ppermute | solution.py:34
  608.4 5.9 collective-permute-start
  616.8 21.2 %collective-permute-start.2 = (bf16[1,4,8,8,128]{4,3,2,1,0:T(8,128)(2,1)S(1)}, bf16[1,4,8,8,128]{4,3,2,1,0:T(8,128)(2,1)S(1)}, u32[]{:S(2)}, u32[]{:S(2)}) collective-permute-start(bf16[1,4,8,8,128]{4,3,2,1,0:T(8,128)(2,1)S(1)} %get-tuple-element.466), channel_id=1, source_target_pairs={{0,64},{64,128},{128,192},{192,256},{256,320},{320,384},{384,448},... | collective-permute-start | bytes 196616 | tf_op jit(solution)/shard_map/while/body/eval_jaxpr/ppermute | solution.py:34
  686.7 5.9 collective-permute-start
  695.1 20.7 %collective-permute-start.2 = (bf16[1,4,8,8,128]{4,3,2,1,0:T(8,128)(2,1)S(1)}, bf16[1,4,8,8,128]{4,3,2,1,0:T(8,128)(2,1)S(1)}, u32[]{:S(2)}, u32[]{:S(2)}) collective-permute-start(bf16[1,4,8,8,128]{4,3,2,1,0:T(8,128)(2,1)S(1)} %get-tuple-element.466), channel_id=1, source_target_pairs={{0,64},{64,128},{128,192},{192,256},{256,320},{320,384},{384,448},... | collective-permute-start | bytes 196616 | tf_op jit(solution)/shard_map/while/body/eval_jaxpr/ppermute | solution.py:34
  764.8 5.9 collective-permute-start
  766.1 4.8 collective-permute-start.1
  773.2 21.2 %collective-permute-start.2 = (bf16[1,4,8,8,128]{4,3,2,1,0:T(8,128)(2,1)S(1)}, bf16[1,4,8,8,128]{4,3,2,1,0:T(8,128)(2,1)S(1)}, u32[]{:S(2)}, u32[]{:S(2)}) collective-permute-start(bf16[1,4,8,8,128]{4,3,2,1,0:T(8,128)(2,1)S(1)} %get-tuple-element.466), channel_id=1, source_target_pairs={{0,64},{64,128},{128,192},{192,256},{256,320},{320,384},{384,448},... | collective-permute-start | bytes 196616 | tf_op jit(solution)/shard_map/while/body/eval_jaxpr/ppermute | solution.py:34
  843.2 5.9 collective-permute-start
  844.5 4.8 collective-permute-start.1
  851.6 20.7 %collective-permute-start.2 = (bf16[1,4,8,8,128]{4,3,2,1,0:T(8,128)(2,1)S(1)}, bf16[1,4,8,8,128]{4,3,2,1,0:T(8,128)(2,1)S(1)}, u32[]{:S(2)}, u32[]{:S(2)}) collective-permute-start(bf16[1,4,8,8,128]{4,3,2,1,0:T(8,128)(2,1)S(1)} %get-tuple-element.466), channel_id=1, source_target_pairs={{0,64},{64,128},{128,192},{192,256},{256,320},{320,384},{384,448},... | collective-permute-start | bytes 196616 | tf_op jit(solution)/shard_map/while/body/eval_jaxpr/ppermute | solution.py:34
  (48 other events, 324.4 us)
Sparse Core Ops, SparseCore 0:
  873.6 268.1 all-reduce.2
where the time goes:
time: 1160 us; the launch traced here: 1150 us
  blocking collectives  488 us (42%)
  waiting for transfers between devices  458 us (39%)
  starting transfers between devices  72.3 us (6%)
  other arithmetic  58.3 us (5%)
  matrix products  32.1 us (3%)
  local copies, waits for them, and re-layouts  17.7 us (2%)
  between operations  14.1 us (1%)
    psum x1, waiting for transfers between devices, per_device(): grads = lax.psum(grads, ('rows', 'dp')) * factor  268 us
    psum x11, blocking collectives, statistics(): total = lax.psum(jnp.sum(grouped * mask_six, axis=(1, 2, 3, 5)), 'rows')  251 us
    psum x11, blocking collectives, statistics(): lax.psum(jnp.sum(centered * centered * mask_six, axis=(1, 2, 3, 5)), 'rows')  237 us
    ppermute x11, waiting for transfers between devices, passed_along(): return lax.ppermute(block, axis, route)  188 us
    ppermute x11, starting transfers between devices, extended_2(): lax.ppermute(tail, axis, [(i, (i + 1) % count) for i in range(ends)])  43.8 us
    dot_general x11, matrix products, tick(): lax.dot_general(patches, masked, (((0,), (0,)), ((), ())), preferred_elem...  24.9 us
  transfers between devices with their start and end apart: 34, of which 23 were waited for; matrix products, arithmetic and copies ran while one was open for 3% of the time, Pallas kernels for 0%

commit v1 on v0

v1 whole, which is shorter than its diff:
```python
import math

import jax
import jax.numpy as jnp
from jax import lax
from jax.experimental import pallas as pl
from jax.experimental.pallas import tpu as pltpu
from jax.sharding import PartitionSpec as P

MESH = pl.DeviceIdType.MESH
EPS = 1e-06
SEGS, ZS, XS, MB, FR, C = 8, 16, 4, 4, 4, 128
WIN = 4
ROWS = 32
CELLS = ROWS * 8
PIECES, PROWS = 14, 64
QROWS = 864
F32, BF16 = jnp.float32, jnp.bfloat16


def group_sum(v):
    lane = lax.broadcasted_iota(jnp.int32, v.shape, 1)
    v = v + jnp.where(lane % 2 == 0, pltpu.roll(v, 127, 1), pltpu.roll(v, 1, 1))
    return v + jnp.where(lane % 4 < 2, pltpu.roll(v, 126, 1), pltpu.roll(v, 2, 1))


def kernel(clips, lengths, w, gain, shift, bias, cot, stash, grad,
           xin, xout, halo, wcat, hs, cotz, rhs, acc, part, xr, zs, zr, st_out, st_in,
           w_sem, cg_s, cg_r, ct_s, ct_r, ss_s, ss_r, rl_s, rl_r, hl_s, hl_r, st_s, st_r,
           xs_s, xs_r, zs_s, zs_r, ag_s, ag_r, xg_s, xg_r):
    seg = lax.axis_index("segment")
    z = lax.axis_index("rows")
    x = lax.axis_index("dp")
    m = z // WIN
    k = z % WIN
    nxt = lax.rem(seg + 1, SEGS)
    prv = lax.rem(seg + SEGS - 1, SEGS)
    first = seg == 0
    last = seg == SEGS - 1

    def dev(s, zz, xx):
        return {"segment": s, "rows": zz, "dp": xx}

    def remote(src, dst, ssem, rsem, target):
        return pltpu.make_async_remote_copy(
            src_ref=src, dst_ref=dst, send_sem=ssem, recv_sem=rsem, device_id=target, device_id_type=MESH)

    def arrived(ref, sem):
        pltpu.make_async_copy(ref, ref, sem).wait()

    w_copies = [
        pltpu.make_async_copy(w.at[pl.ds(a * 9 * C, 9 * C)], wcat.at[:, pl.ds(a * C, C)], w_sem.at[a])
        for a in range(3)
    ]
    for cp in w_copies:
        cp.start()

    bar = pltpu.get_barrier_semaphore()

    def greet(target):
        pl.semaphore_signal(bar, inc=1, device_id=target, device_id_type=MESH)

    for o in range(1, ZS):
        greet(dev(seg, lax.rem(z + o, ZS), x))
    for o in range(1, XS):
        greet(dev(seg, z, lax.rem(x + o, XS)))
    for kk in range(WIN):
        greet(dev(nxt, m * WIN + kk, x))
        greet(dev(prv, m * WIN + kk, x))
    pl.semaphore_wait(bar, ZS - 1 + XS - 1 + 2 * WIN)

    def regroup(src, dst, ssem, rsem):
        for i in range(MB):
            to = i * WIN + m
            here = dst.at[:, pl.ds(pl.multiple_of(k * 64, 64), 64)]

            @pl.when(to != z)
            def _():
                remote(src.at[i], here, ssem.at[i], rsem.at[k], dev(seg, to, x)).start()

            @pl.when(to == z)
            def _():
                pltpu.make_async_copy(src.at[i], here, rsem.at[k]).start()

    def regroup_recv(dst, rsem):
        for j in range(WIN):
            arrived(dst.at[:, pl.ds(j * 64, 64)], rsem.at[j])

    def regroup_sent(src, ssem):
        for i in range(MB):
            @pl.when(i * WIN + m != z)
            def _():
                arrived(src.at[i], ssem.at[i])

    length = lengths[m, 0]
    mask = [jnp.where(f < length, 1.0, 0.0).astype(F32) for f in range(FR)]
    n_dev = (length * CELLS).astype(F32)

    def local_sums(ref):
        total = jnp.zeros((8, C), F32)
        for f in range(FR):
            v = ref[f].astype(F32).reshape(ROWS, 8, C)
            total = total + jnp.sum(v, axis=0) * mask[f]
        return jnp.broadcast_to(jnp.sum(total, axis=0, keepdims=True), (8, C))

    def local_stats(ref):
        sums = local_sums(ref)
        mean = (sums / n_dev)[None]
        total = jnp.zeros((8, C), F32)
        for f in range(FR):
            v = ref[f].astype(F32).reshape(ROWS, 8, C) - mean
            total = total + jnp.sum(v * v, axis=0) * mask[f]
        st_out[0] = sums
        st_out[1] = jnp.broadcast_to(jnp.sum(total, axis=0, keepdims=True), (8, C))

    def edge_copies(ref, to):
        up = remote(ref.at[:, pl.ds(0, 16)], halo.at[1], hl_s.at[0], hl_r.at[1], dev(to, z - 1, x))
        down = remote(ref.at[:, pl.ds(CELLS - 16, 16)], halo.at[0], hl_s.at[1], hl_r.at[0], dev(to, z + 1, x))
        return up, down

    def send_edges(ref, to):
        @pl.when(k > 0)
        def _():
            edge_copies(ref, to)[0].start()

        @pl.when(k < WIN - 1)
        def _():
            edge_copies(ref, to)[1].start()

    def edges_sent(ref):
        @pl.when(k > 0)
        def _():
            arrived(ref.at[:, pl.ds(0, 16)], hl_s.at[0])

        @pl.when(k < WIN - 1)
        def _():
            arrived(ref.at[:, pl.ds(CELLS - 16, 16)], hl_s.at[1])

    @pl.when(k == 0)
    def _():
        halo[0] = jnp.zeros((FR, 16, C), BF16)

    @pl.when(k == WIN - 1)
    def _():
        halo[1] = jnp.zeros((FR, 16, C), BF16)

    @pl.when(first)
    def _():
        regroup(clips, xin, cg_s, cg_r)
        regroup_recv(xin, cg_r)
        send_edges(xin, seg)
        local_stats(xin)
        for o in range(1, WIN):
            remote(st_out, st_in.at[k], st_s.at[o], st_r.at[k], dev(seg, m * WIN + lax.rem(k + o, WIN), x)).start()
        st_in[k] = st_out[...]
        regroup_sent(clips, cg_s)
        for o in range(1, WIN):
            arrived(st_out, st_s.at[o])
        edges_sent(xin)

    @pl.when(seg > 1)
    def _():
        regroup(cot, cotz, ct_s, ct_r)

    @pl.when(seg > 0)
    def _():
        for h in range(2):
            arrived(xin.at[:, pl.ds(h * 128, 128)], rl_r.at[h])

    @pl.when(seg <= 1)
    def _():
        regroup(cot, cotz, ct_s, ct_r)

    @pl.when(k > 0)
    def _():
        arrived(halo.at[0], hl_r.at[0])

    @pl.when(k < WIN - 1)
    def _():
        arrived(halo.at[1], hl_r.at[1])

    for kk in range(WIN):
        @pl.when(jnp.logical_or(seg > 0, k != kk))
        def _():
            arrived(st_in.at[kk], st_r.at[kk])

    total = st_in[0, 0] + st_in[1, 0] + st_in[2, 0] + st_in[3, 0]
    count = n_dev * (4.0 * WIN)
    mean = group_sum(total) / count
    spread = jnp.zeros((8, C), F32)
    for kk in range(WIN):
        off = st_in[kk, 0] / n_dev - mean
        spread = spread + st_in[kk, 1] + n_dev * (off * off)
    rstd = lax.rsqrt(group_sum(spread) / count + EPS)
    scale = rstd * gain[...]
    offset = jnp.broadcast_to(shift[...], (8, C))
    col = lax.broadcasted_iota(jnp.int32, (1, 8, C), 1)

    def act(v):
        v = (v - mean[None]) * scale[None] + offset[None]
        return v / (1.0 + jnp.exp(-v))

    def put(row, n, per_frame):
        for fp in range(2):
            pair = [per_frame[2 * fp], per_frame[2 * fp + 1]]
            for d in range(3):
                if d == 0:
                    out = [jnp.where(col == 0, 0.0, pltpu.roll(h.reshape(n * 8, C), 1, 0).reshape(n, 8, C)) for h in pair]
                elif d == 2:
                    out = [jnp.where(col == 7, 0.0, pltpu.roll(h.reshape(n * 8, C), n * 8 - 1, 0).reshape(n, 8, C)) for h in pair]
                else:
                    out = pair
                hs[d, pl.ds(row, n), fp] = jnp.concatenate(out, axis=1).astype(BF16)

    top_here, bottom_here = k > 0, k < WIN - 1
    put(0, 1, [jnp.where(top_here, act(halo[0, f, 8:16].astype(F32).reshape(1, 8, C)), 0.0) for f in range(FR)])
    put(ROWS + 1, 1, [jnp.where(bottom_here, act(halo[1, f, 0:8].astype(F32).reshape(1, 8, C)), 0.0) for f in range(FR)])

    def norm_step(j, c):
        put(8 * j + 1, 8, [
            act(xin[f, pl.ds(pl.multiple_of(j * 64, 64), 64)].astype(F32).reshape(8, 8, C)) for f in range(FR)])
        return c

    lax.fori_loop(0, ROWS // 8, norm_step, 0)

    for cp in w_copies:
        cp.wait()

    bias_row = bias[...].reshape(1, 1, C)
    half = ROWS // 2
    for h in range(2):
        def taps(fp):
            return jnp.concatenate(
                [hs[d, pl.ds(h * half + b, half), fp].reshape(half * 16, C) for b in range(3) for d in range(3)], axis=1)

        p01 = jnp.dot(taps(0), wcat[...], preferred_element_type=F32).reshape(half, 2, 8, 3 * C)
        p23 = jnp.dot(taps(1), wcat[:, C:], preferred_element_type=F32).reshape(half, 2, 8, 2 * C)
        a0, a1, a2 = slice(0, C), slice(C, 2 * C), slice(2 * C, 3 * C)
        early = p01[:, 0, :, a0] + p01[:, 0, :, a1]
        outs = [
            early + p01[:, 0, :, a2],
            early + p01[:, 1, :, a2],
            p01[:, 0, :, a0] + p01[:, 1, :, a1] + p23[:, 0, :, a1],
            p01[:, 1, :, a0] + p23[:, 0, :, a0] + p23[:, 1, :, a1],
        ]
        for f in range(FR):
            v = xin[f, h * 128:(h + 1) * 128].astype(F32).reshape(half, 8, C)
            out = (v + outs[f] + bias_row) * mask[f]
            xout[f, h * 128:(h + 1) * 128] = out.reshape(128, C).astype(BF16)

        @pl.when(jnp.logical_not(last))
        def _():
            part_h = (slice(None), pl.ds(h * 128, 128))
            remote(xout.at[part_h], xin.at[part_h], rl_s.at[h], rl_r.at[h], dev(nxt, z, x)).start()

    @pl.when(jnp.logical_not(last))
    def _():
        send_edges(xout, nxt)
        local_stats(xout)
        for kk in range(WIN):
            remote(st_out, st_in.at[k], st_s.at[kk], st_r.at[k], dev(nxt, m * WIN + kk, x)).start()

    for j in range(WIN):
        to = k * WIN + j
        src = xout.at[:, pl.ds(j * 64, 64)]

        @pl.when(to != z)
        def _():
            remote(src, stash.at[m], ss_s.at[j], ss_r.at[m], dev(seg, to, x)).start()

        @pl.when(to == z)
        def _():
            pltpu.make_async_copy(src, stash.at[m], ss_r.at[m]).start()

    regroup_recv(cotz, ct_r)

    def rhs_step(j, c):
        cut = pl.ds(pl.multiple_of(j * 64, 64), 64)
        cs = [cotz[f, cut].astype(F32).reshape(8, 8, C) * mask[f] for f in range(FR)]
        zero = jnp.zeros((8, 8, C), F32)
        two = cs[0] + cs[1]
        cols = [
            [[two + cs[2], cs[3]], [zero, zero]],
            [[two, cs[2]], [cs[3], zero]],
            [[cs[0], cs[1]], [cs[2], cs[3]]],
        ]
        for a in range(3):
            for fp in range(2):
                rhs[pl.ds(8 * j, 8), fp, :, a * C:(a + 1) * C] = jnp.concatenate(cols[a][fp], axis=1).astype(BF16)
        return c

    lax.fori_loop(0, ROWS // 8, rhs_step, 0)
    factor = 1.0 / math.sqrt(MB * XS * FR * 128 * 8)
    for b in range(3):
        lhs = jnp.concatenate([hs[d, b:b + ROWS].reshape(ROWS * 32, C) for d in range(3)], axis=1)
        acc[b * 3 * C:(b + 1) * 3 * C] = lax.dot_general(
            lhs, rhs[...].reshape(ROWS * 32, 3 * C), (((0,), (0,)), ((), ())), preferred_element_type=F32)
    for blk in range(12):
        a, i = blk // 4, blk % 4
        part[blk // 3, (blk % 3) * 288:(blk % 3 + 1) * 288] = (
            acc[i * 288:(i + 1) * 288, a * C:(a + 1) * C] * factor).astype(BF16)
    for q in range(4):
        part[q, QROWS:] = jnp.zeros((PIECES * PROWS - QROWS, C), BF16)

    for o in (2, 1, 3):
        to = lax.rem(x + o, XS)
        remote(part.at[to], xr.at[o - 1], xs_s.at[o - 1], xs_r.at[o - 1], dev(seg, z, to)).start()
    for o in (1, 3, 2):
        arrived(xr.at[o - 1], xs_r.at[o - 1])

    def x_sum(p, c):
        cut = pl.ds(pl.multiple_of(p * PROWS, PROWS), PROWS)
        v = part[x, cut].astype(F32)
        for o in range(3):
            v = v + xr[o, cut].astype(F32)
        zs[p] = v.astype(BF16)
        return c

    lax.fori_loop(0, PIECES, x_sum, 0)

    order = (8, 7, 9, 6, 10, 5, 11, 4, 12, 3, 13, 2, 14, 1, 15)
    for o in order:
        to = lax.rem(z + o, ZS)

        @pl.when(to < PIECES)
        def _():
            remote(zs.at[to], zr.at[o - 1], zs_s.at[o - 1], zs_r.at[o - 1], dev(seg, to, x)).start()

    @pl.when(z < PIECES)
    def _():
        v = zs[z].astype(F32)
        for o in order[::-1]:
            arrived(zr.at[o - 1], zs_r.at[o - 1])
            v = v + zr[o - 1].astype(F32)
        grad[x, z] = v.astype(BF16)
        for o in order:
            remote(grad.at[x, z], grad.at[x, z], ag_s.at[o - 1], ag_r.at[o - 1], dev(seg, lax.rem(z + o, ZS), x)).start()

    for o in order[::-1]:
        src_z = lax.rem(z + ZS - o, ZS)

        @pl.when(src_z < PIECES)
        def _():
            arrived(grad.at[x, src_z], ag_r.at[o - 1])

    for o in (2, 1, 3):
        remote(grad.at[x], grad.at[x], xg_s.at[o - 1], xg_r.at[o - 1], dev(seg, z, lax.rem(x + o, XS))).start()

    for j in range(MB):
        arrived(stash.at[j], ss_r.at[j])
    for j in range(WIN):
        @pl.when(k * WIN + j != z)
        def _():
            arrived(xout.at[:, pl.ds(j * 64, 64)], ss_s.at[j])

    regroup_sent(cot, ct_s)

    @pl.when(jnp.logical_not(last))
    def _():
        for h in range(2):
            arrived(xout.at[:, pl.ds(h * 128, 128)], rl_s.at[h])
        for kk in range(WIN):
            arrived(st_out, st_s.at[kk])
        edges_sent(xout)

    for o in range(1, XS):
        arrived(part.at[0], xs_s.at[o - 1])
    for o in range(1, ZS):
        @pl.when(lax.rem(z + o, ZS) < PIECES)
        def _():
            arrived(zs.at[0], zs_s.at[o - 1])

    @pl.when(z < PIECES)
    def _():
        for o in range(1, ZS):
            arrived(zr.at[0], ag_s.at[o - 1])

    for o in range(1, XS):
        arrived(grad.at[lax.rem(x + XS - o, XS)], xg_r.at[o - 1])
        arrived(grad.at[x], xg_s.at[o - 1])


def per_device(clips, lengths, conv_weight, norm_gain, norm_shift, conv_bias, cotangent):
    vmem, anyspace = pltpu.VMEM, pl.ANY
    dma = pltpu.SemaphoreType.DMA
    stash, grad = pl.pallas_call(
        kernel,
        out_shape=(
            jax.ShapeDtypeStruct((MB, FR, 64, C), BF16),
            jax.ShapeDtypeStruct((XS, PIECES, PROWS, C), BF16),
        ),
        in_specs=[
            pl.BlockSpec(memory_space=vmem),
            pl.BlockSpec(memory_space=pltpu.SMEM),
            pl.BlockSpec(memory_space=anyspace),
            pl.BlockSpec(memory_space=vmem),
            pl.BlockSpec(memory_space=vmem),
            pl.BlockSpec(memory_space=vmem),
            pl.BlockSpec(memory_space=vmem),
        ],
        out_specs=(pl.BlockSpec(memory_space=vmem), pl.BlockSpec(memory_space=vmem)),
        scratch_shapes=[
            vmem((FR, CELLS, C), BF16),
            vmem((FR, CELLS, C), BF16),
            vmem((2, FR, 16, C), BF16),
            vmem((9 * C, 3 * C), BF16),
            vmem((3, ROWS + 2, 2, 16, C), BF16),
            vmem((FR, CELLS, C), BF16),
            vmem((ROWS, 2, 16, 3 * C), BF16),
            vmem((9 * C, 3 * C), F32),
            vmem((XS, PIECES * PROWS, C), BF16),
            vmem((XS - 1, PIECES * PROWS, C), BF16),
            vmem((PIECES, PROWS, C), BF16),
            vmem((ZS - 1, PROWS, C), BF16),
            vmem((2, 8, C), F32),
            vmem((WIN, 2, 8, C), F32),
            dma((3,)),
            dma((4,)), dma((4,)), dma((4,)), dma((4,)), dma((4,)), dma((4,)),
            dma((2,)), dma((2,)), dma((2,)), dma((2,)), dma((4,)), dma((4,)),
            dma((3,)), dma((3,)), dma((15,)), dma((15,)), dma((15,)), dma((15,)), dma((3,)), dma((3,)),
        ],
        compiler_params=pltpu.CompilerParams(
            collective_id=0, has_side_effects=True, vmem_limit_bytes=48 * 2**20),
        cost_estimate=pl.CostEstimate(flops=2 * 10**9, bytes_accessed=4 * 10**6, transcendentals=10**6),
    )(
        clips.reshape(MB, FR, 64, C), lengths, conv_weight[0], norm_gain, norm_shift, conv_bias,
        cotangent.reshape(MB, FR, 64, C))
    grads = grad.reshape(XS, PIECES * PROWS, C)[:, :QROWS].reshape(27 * C, C).astype(F32)
    return stash.reshape(1, MB, 1, FR, 8, 8, C), grads[None]


def solution(mesh):
    in_specs = (
        P(None, "dp", None, "rows", None, None),
        P(None, "dp"),
        P("segment", None, None),
        P("segment", None),
        P("segment", None),
        P("segment", None),
        P("segment", None, "dp", None, "rows", None, None),
    )
    out_specs = (P("segment", None, "dp", None, "rows", None, None), P("segment", None, None))
    return jax.shard_map(per_device, mesh=mesh, in_specs=in_specs, out_specs=out_specs, check_vma=False)
```

time: 1160 us -> 151 us (0.13)
  blocking collectives: 488 us -> 0 us
  waiting for transfers between devices: 458 us -> 0 us
  Pallas kernels: 0 us -> 142 us
  starting transfers between devices: 72.3 us -> 0 us
  other arithmetic: 58.3 us -> 1.32 us
  matrix products: 32.1 us -> 0 us
  between operations: 14.1 us -> 0.65 us
    psum x22 -> x0, blocking collectives: 488 us -> none  [the longest x11 251 us: statistics(): total = lax.psum(jnp.sum(grouped * mask_six, axis=(1, 2, 3, 5)), 'rows')]
    psum x1 -> x0, waiting for transfers between devices: 268 us -> none  [per_device(): grads = lax.psum(grads, ('rows', 'dp')) * factor]
    ppermute x33 -> x0, waiting for transfers between devices: 190 us -> none  [the longest x11 188 us: passed_along(): return lax.ppermute(block, axis, route)]
    pallas_call x0 -> x1, Pallas kernels: none -> 142 us  [per_device(): pl.pallas_call(kernel, out_shape=(jax.ShapeDtypeStruct((MB, FR, 64, C), B...]
    ppermute x33 -> x0, starting transfers between devices: 72.3 us -> none  [the longest x11 43.8 us: extended_2(): lax.ppermute(tail, axis, [(i, (i + 1) % count) for i in range(ends)])]
    dot_general x22 -> x0, matrix products: 32.1 us -> none  [the longest x11 24.9 us: tick(): lax.dot_general(patches, masked, (((0,), (0,)), ((), ())), preferred_elem...]
    convert_element_type x33 -> x1, other arithmetic: 20.5 us -> 1.32 us  [per_device(): grad.reshape(XS, PIECES * PROWS, C)[:, :QROWS].reshape(27 * C, C)]
    reduce_sum x44 -> x0, other arithmetic: 14.4 us -> none  [the longest x22 11.8 us: statistics(): total = lax.psum(jnp.sum(grouped * mask_six, axis=(1, 2, 3, 5)), 'rows')]
  transfers between devices with their start and end apart: 34 -> 0, of which waited for: 23 -> 0; matrix products, arithmetic and copies ran while one was open for 3% -> 0% of each run, Pallas kernels for 0% -> 0%
where the time goes in v1:
time: 151 us; the launch traced here: 150 us
  Pallas kernels  142 us (94%)
  local copies, waits for them, and re-layouts  6.53 us (4%)
    pallas_call x1, Pallas kernels, per_device(): pl.pallas_call(kernel, out_shape=(jax.ShapeDtypeStruct((MB, FR, 64, C), B...  142 us
    unnamed x14, local copies, waits for them, and re-layouts  6.47 us

profile of v1, /device:TPU:25, one launch (start us, length us, event | category | flops | bytes accessed | tf_op | source)
XLA Modules:
  0.0 150.3 jit_solution(17286541737406428981)
XLA Ops:
  0.6 0.7 copy.9.lengths
  1.4 0.0 copy-start
  1.4 1.2 copy-done
  2.5 0.0 copy-start.1
  2.5 0.9 copy-done.1
  3.5 0.0 copy-start.2
  3.5 0.9 copy-done.2
  4.4 0.0 copy-start.3
  4.4 0.7 copy-done.3
  5.1 0.0 copy-start.4
  5.1 0.7 copy-done.4
  5.8 0.0 copy-start.5
  5.8 0.7 copy-done.5
  6.4 141.7 %shard_map.86 = (bf16[4,4,64,128]{3,2,1,0:T(8,128)(2,1)S(1)}, bf16[4,14,64,128]{3,2,1,0:T(8,128)(2,1)S(1)}) custom-call(bf16[4,4,64,128]{3,2,1,0:T(8,128)(2,1)S(1)} %bitcast.14, s32[4,1]{1,0:T(4,128)S(1)} %copy.9.lengths, bf16[3456,128]{1,0:T(8,128)(2,1)S(1)} %bitcast.13, f32[1,128]{1,0:T(1,128)S(1)} %copy-done.3, f32[1,128]{1,0:T(1,128)S(1)} %copy-done.4, ...), custom_call_target="tpu_custom_call" | custom-call | flops 2000000000 | bytes 4000000 | tf_op jit(solution)/shard_map/pallas_call | solution.py:386
  148.2 0.1 slice.4
  148.2 1.3 bitcast_convert_fusion
  149.5 0.7 copy.12
Async XLA Ops:
  1.4 1.2 copy-start
  2.5 0.9 copy-start.1
  3.5 0.9 copy-start.2
  4.4 0.7 copy-start.3
  5.1 0.7 copy-start.4
  5.8 0.7 copy-start.5

commit v2 on v1

v2 whole, which is shorter than its diff:
```python
import math

import jax
import jax.numpy as jnp
from jax import lax
from jax.experimental import pallas as pl
from jax.experimental.pallas import tpu as pltpu
from jax.sharding import PartitionSpec as P

MESH = pl.DeviceIdType.MESH
EPS = 1e-06
SEGS, ZS, XS, MB, FR, C = 8, 16, 4, 4, 4, 128
WIN = 4
ROWS = 32
CELLS = ROWS * 8
CH, PC, PR = 3, 9, 32
F32, BF16 = jnp.float32, jnp.bfloat16


def group_sum(v):
    lane = lax.broadcasted_iota(jnp.int32, v.shape, 1)
    v = v + jnp.where(lane % 2 == 0, pltpu.roll(v, 127, 1), pltpu.roll(v, 1, 1))
    return v + jnp.where(lane % 4 < 2, pltpu.roll(v, 126, 1), pltpu.roll(v, 2, 1))


def kernel(clips_any, lengths_any, w, gain_any, shift_any, bias_any, cot, stash, grad,
           clips, lengths, gain, shift, bias,
           xin, xout, halo, wcat, hs, cotz, rhs, part, xr, zs, zr, st_out, st_in, st_clip, norm, go,
           in_sem, w_sem, cg_s, cg_r, ct_s, ct_r, ss_s, ss_r, rl_s, rl_r, hl_s, hl_r, st_s, st_r,
           sc_s, sc_r,
           xs_s, xs_r, zs_s, zs_r, ag_s, ag_r, xg_s, xg_r):
    seg = lax.axis_index("segment")
    z = lax.axis_index("rows")
    x = lax.axis_index("dp")
    m = z // WIN
    k = z % WIN
    nxt = lax.rem(seg + 1, SEGS)
    prv = lax.rem(seg + SEGS - 1, SEGS)
    first = seg == 0
    last = seg == SEGS - 1

    def dev(s, zz, xx):
        return {"segment": s, "rows": zz, "dp": xx}

    def remote(src, dst, ssem, rsem, target):
        return pltpu.make_async_remote_copy(
            src_ref=src, dst_ref=dst, send_sem=ssem, recv_sem=rsem, device_id=target, device_id_type=MESH)

    def arrived(ref, sem):
        pltpu.make_async_copy(ref, ref, sem).wait()

    in_copies = [
        pltpu.make_async_copy(src, dst, in_sem.at[i])
        for i, (src, dst) in enumerate([
            (clips_any, clips), (lengths_any, lengths), (gain_any, gain), (shift_any, shift), (bias_any, bias)])
    ]
    for cp in in_copies:
        cp.start()

    w_copies = [
        pltpu.make_async_copy(w.at[pl.ds(a * 9 * C, 9 * C)], wcat.at[:, pl.ds(a * C, C)], w_sem.at[a])
        for a in range(3)
    ]
    for cp in w_copies:
        cp.start()

    bar = pltpu.get_barrier_semaphore()

    def greet(target):
        pl.semaphore_signal(bar, inc=1, device_id=target, device_id_type=MESH)

    for o in range(1, ZS):
        greet(dev(seg, lax.rem(z + o, ZS), x))
    for o in range(1, XS):
        greet(dev(seg, z, lax.rem(x + o, XS)))
    for kk in range(WIN):
        greet(dev(nxt, m * WIN + kk, x))
        greet(dev(prv, m * WIN + kk, x))
    for cp in in_copies:
        cp.wait()
    pl.semaphore_wait(bar, ZS - 1 + XS - 1 + 2 * WIN)

    def regroup(src, dst, ssem, rsem):
        for i in range(MB):
            to = i * WIN + m
            here = dst.at[:, pl.ds(pl.multiple_of(k * 64, 64), 64)]

            @pl.when(to != z)
            def _():
                remote(src.at[i], here, ssem.at[i], rsem.at[k], dev(seg, to, x)).start()

            @pl.when(to == z)
            def _():
                pltpu.make_async_copy(src.at[i], here, rsem.at[k]).start()

    def regroup_recv(dst, rsem):
        for j in range(WIN):
            arrived(dst.at[:, pl.ds(j * 64, 64)], rsem.at[j])

    def regroup_sent(src, ssem):
        for i in range(MB):
            @pl.when(i * WIN + m != z)
            def _():
                arrived(src.at[i], ssem.at[i])

    length = lengths[m, 0]
    mask = [jnp.where(f < length, 1.0, 0.0).astype(F32) for f in range(FR)]
    n_dev = (length * CELLS).astype(F32)

    def stats_of(ref, rows, masks, n):
        def over(fn):
            total = jnp.zeros((8, C), F32)
            for f in range(FR):
                total = total + jnp.sum(fn(ref[f].astype(F32).reshape(rows, 8, C)), axis=0) * masks[f]
            return jnp.broadcast_to(jnp.sum(total, axis=0, keepdims=True), (8, C))

        sums = over(lambda v: v)
        mean = (sums / n)[None]
        return sums, over(lambda v: (v - mean) * (v - mean))

    def combine(parts, n):
        count = n * (4.0 * len(parts))
        total = parts[0][0]
        for sums, _ in parts[1:]:
            total = total + sums
        mean = group_sum(total) / count
        spread = jnp.zeros((8, C), F32)
        for sums, squares in parts:
            off = sums / n - mean
            spread = spread + squares + n * (off * off)
        norm[0] = mean
        norm[1] = lax.rsqrt(group_sum(spread) / count + EPS)

    def send_edges(ref, to):
        @pl.when(k > 0)
        def _():
            remote(ref.at[:, pl.ds(0, 16)], halo.at[1], hl_s.at[0], hl_r.at[1], dev(to, z - 1, x)).start()

        @pl.when(k < WIN - 1)
        def _():
            remote(ref.at[:, pl.ds(CELLS - 16, 16)], halo.at[0], hl_s.at[1], hl_r.at[0], dev(to, z + 1, x)).start()

    def edges_sent(ref):
        @pl.when(k > 0)
        def _():
            arrived(ref.at[:, pl.ds(0, 16)], hl_s.at[0])

        @pl.when(k < WIN - 1)
        def _():
            arrived(ref.at[:, pl.ds(CELLS - 16, 16)], hl_s.at[1])

    @pl.when(k == 0)
    def _():
        halo[0] = jnp.zeros((FR, 16, C), BF16)

    @pl.when(k == WIN - 1)
    def _():
        halo[1] = jnp.zeros((FR, 16, C), BF16)

    def post(src, dst, ssem, rsem, to):
        @pl.when(to != z)
        def _():
            remote(src, dst, ssem, rsem, dev(seg, to, x)).start()

        @pl.when(to == z)
        def _():
            pltpu.make_async_copy(src, dst, rsem).start()

    def posted(src, ssem, to):
        @pl.when(to != z)
        def _():
            arrived(src, ssem)

    low, high = clips.at[:, :, pl.ds(0, 16)], clips.at[:, :, pl.ds(48, 16)]
    goes_up = jnp.logical_and(k == 0, m > 0)
    goes_down = jnp.logical_and(k == WIN - 1, m < WIN - 1)

    @pl.when(first)
    def _():
        regroup(clips, xin, cg_s, cg_r)
        for i in range(MB):
            @pl.when(goes_up)
            def _():
                post(low.at[i], halo.at[1], sc_s.at[16 + i], hl_r.at[1], i * WIN + m - 1)

            @pl.when(goes_down)
            def _():
                post(high.at[i], halo.at[0], sc_s.at[16 + i], hl_r.at[0], i * WIN + m + 1)

        for i in range(MB):
            here = lengths[i, 0]
            masks = [jnp.where(f < here, 1.0, 0.0).astype(F32) for f in range(FR)]
            st_clip[i, 0], st_clip[i, 1] = stats_of(clips.at[i], 8, masks, (here * 64).astype(F32))
            for kk in range(WIN):
                post(st_clip.at[i], st_in.at[z], sc_s.at[i * WIN + kk], sc_r.at[z], i * WIN + kk)

        regroup_recv(xin, cg_r)
        for j in range(ZS):
            arrived(st_in.at[j], sc_r.at[j])
        combine([(st_in[j, 0], st_in[j, 1]) for j in range(ZS)], (length * 64).astype(F32))

    @pl.when(seg > 1)
    def _():
        regroup(cot, cotz, ct_s, ct_r)

    @pl.when(seg > 0)
    def _():
        for h in range(2):
            arrived(xin.at[:, pl.ds(h * 128, 128)], rl_r.at[h])
        for kk in range(WIN):
            arrived(st_in.at[kk], st_r.at[kk])
        combine([(st_in[kk, 0], st_in[kk, 1]) for kk in range(WIN)], n_dev)

    @pl.when(k > 0)
    def _():
        arrived(halo.at[0], hl_r.at[0])

    @pl.when(k < WIN - 1)
    def _():
        arrived(halo.at[1], hl_r.at[1])

    mean = norm[0]
    scale = norm[1] * gain[...]
    offset = jnp.broadcast_to(shift[...], (8, C))
    col = lax.broadcasted_iota(jnp.int32, (1, 8, C), 1)

    def act(v):
        v = (v - mean[None]) * scale[None] + offset[None]
        return v / (1.0 + jnp.exp(-v))

    def put(row, n, per_frame):
        for fp in range(2):
            pair = [per_frame[2 * fp], per_frame[2 * fp + 1]]
            for d in range(3):
                if d == 0:
                    out = [jnp.where(col == 0, 0.0, pltpu.roll(h.reshape(n * 8, C), 1, 0).reshape(n, 8, C)) for h in pair]
                elif d == 2:
                    out = [jnp.where(col == 7, 0.0, pltpu.roll(h.reshape(n * 8, C), n * 8 - 1, 0).reshape(n, 8, C)) for h in pair]
                else:
                    out = pair
                hs[d, pl.ds(row, n), fp] = jnp.concatenate(out, axis=1).astype(BF16)

    top_here, bottom_here = k > 0, k < WIN - 1
    put(0, 1, [jnp.where(top_here, act(halo[0, f, 8:16].astype(F32).reshape(1, 8, C)), 0.0) for f in range(FR)])
    put(ROWS + 1, 1, [jnp.where(bottom_here, act(halo[1, f, 0:8].astype(F32).reshape(1, 8, C)), 0.0) for f in range(FR)])

    def norm_step(j, c):
        put(8 * j + 1, 8, [
            act(xin[f, pl.ds(pl.multiple_of(j * 64, 64), 64)].astype(F32).reshape(8, 8, C)) for f in range(FR)])
        return c

    lax.fori_loop(0, ROWS // 8, norm_step, 0)

    for cp in w_copies:
        cp.wait()

    factor = 1.0 / math.sqrt(MB * XS * FR * 128 * 8)

    def gradient():
        regroup_recv(cotz, ct_r)

        def rhs_step(j, c):
            cut = pl.ds(pl.multiple_of(j * 64, 64), 64)
            cs = [cotz[f, cut].astype(F32).reshape(8, 8, C) * mask[f] for f in range(FR)]
            zero = jnp.zeros((8, 8, C), F32)
            two = cs[0] + cs[1]
            cols = [
                [[two + cs[2], cs[3]], [zero, zero]],
                [[two, cs[2]], [cs[3], zero]],
                [[cs[0], cs[1]], [cs[2], cs[3]]],
            ]
            for a in range(3):
                for fp in range(2):
                    rhs[pl.ds(8 * j, 8), fp, :, a * C:(a + 1) * C] = jnp.concatenate(cols[a][fp], axis=1).astype(BF16)
            return c

        lax.fori_loop(0, ROWS // 8, rhs_step, 0)
        for b in range(CH):
            lhs = jnp.concatenate([hs[d, b:b + ROWS].reshape(ROWS * 32, C) for d in range(3)], axis=1)
            acc = lax.dot_general(
                lhs, rhs[...].reshape(ROWS * 32, 3 * C), (((0,), (0,)), ((), ())), preferred_element_type=F32)
            for a in range(3):
                block = (acc[:, a * C:(a + 1) * C] * factor).astype(BF16)
                for q in range(XS):
                    part[b, q, 3 * a:3 * a + 3] = block[96 * q:96 * q + 96].reshape(3, PR, C)
            for o in (2, 1, 3):
                to = lax.rem(x + o, XS)
                remote(part.at[b, to], xr.at[b, o - 1], xs_s.at[b, o - 1], xs_r.at[b, o - 1],
                       dev(seg, z, to)).start()

    @pl.when(last)
    def _():
        gradient()

    bias_row = bias[...].reshape(1, 1, C)
    half = ROWS // 2
    for h in range(2):
        def taps(fp):
            return jnp.concatenate(
                [hs[d, pl.ds(h * half + b, half), fp].reshape(half * 16, C) for b in range(3) for d in range(3)], axis=1)

        p01 = jnp.dot(taps(0), wcat[...], preferred_element_type=F32).reshape(half, 2, 8, 3 * C)
        p23 = jnp.dot(taps(1), wcat[:, C:], preferred_element_type=F32).reshape(half, 2, 8, 2 * C)
        a0, a1, a2 = slice(0, C), slice(C, 2 * C), slice(2 * C, 3 * C)
        early = p01[:, 0, :, a0] + p01[:, 0, :, a1]
        outs = [
            early + p01[:, 0, :, a2],
            early + p01[:, 1, :, a2],
            p01[:, 0, :, a0] + p01[:, 1, :, a1] + p23[:, 0, :, a1],
            p01[:, 1, :, a0] + p23[:, 0, :, a0] + p23[:, 1, :, a1],
        ]
        for f in range(FR):
            v = xin[f, h * 128:(h + 1) * 128].astype(F32).reshape(half, 8, C)
            out = (v + outs[f] + bias_row) * mask[f]
            xout[f, h * 128:(h + 1) * 128] = out.reshape(128, C).astype(BF16)

        @pl.when(jnp.logical_not(last))
        def _():
            part_h = (slice(None), pl.ds(h * 128, 128))
            remote(xout.at[part_h], xin.at[part_h], rl_s.at[h], rl_r.at[h], dev(nxt, z, x)).start()

    @pl.when(jnp.logical_not(last))
    def _():
        send_edges(xout, nxt)
        st_out[0], st_out[1] = stats_of(xout, ROWS, mask, n_dev)
        for kk in range(WIN):
            remote(st_out, st_in.at[k], st_s.at[kk], st_r.at[k], dev(nxt, m * WIN + kk, x)).start()

    @pl.when(jnp.logical_and(seg % 2 == 1, jnp.logical_not(last)))
    def _():
        pl.semaphore_signal(go, inc=1, device_id=dev(seg - 1, z, x), device_id_type=MESH)

    @pl.when(jnp.logical_and(seg % 2 == 0, seg < SEGS - 2))
    def _():
        pl.semaphore_wait(go, 1)

    @pl.when(seg <= 1)
    def _():
        regroup(cot, cotz, ct_s, ct_r)

    for j in range(WIN):
        to = k * WIN + j
        src = xout.at[:, pl.ds(j * 64, 64)]

        @pl.when(to != z)
        def _():
            remote(src, stash.at[m], ss_s.at[j], ss_r.at[m], dev(seg, to, x)).start()

        @pl.when(to == z)
        def _():
            pltpu.make_async_copy(src, stash.at[m], ss_r.at[m]).start()

    @pl.when(jnp.logical_not(last))
    def _():
        gradient()

    order = (8, 7, 9, 6, 10, 5, 11, 4, 12, 3, 13, 2, 14, 1, 15)

    def piece(c, zz):
        return lax.rem(zz + 2 * ZS - PC * c, ZS)

    for c in range(CH):
        for o in (1, 3, 2):
            arrived(xr.at[c, o - 1], xs_r.at[c, o - 1])
        for p in range(PC):
            v = part[c, x, p].astype(F32)
            for o in range(3):
                v = v + xr[c, o, p].astype(F32)
            zs[c, p] = v.astype(BF16)
        for o in order:
            to = lax.rem(z + o, ZS)
            p_to = piece(c, to)

            @pl.when(p_to < PC)
            def _():
                remote(zs.at[c, p_to], zr.at[c, o - 1], zs_s.at[c, o - 1], zs_r.at[c, o - 1], dev(seg, to, x)).start()

    for c in range(CH):
        mine = piece(c, z)

        @pl.when(mine < PC)
        def _():
            v = zs[c, mine].astype(F32)
            for o in order[::-1]:
                arrived(zr.at[c, o - 1], zs_r.at[c, o - 1])
                v = v + zr[c, o - 1].astype(F32)
            kept = grad.at[mine // 3, c, 3 * x + mine % 3]
            kept[...] = v.astype(BF16)
            for o in order:
                remote(kept, kept, ag_s.at[c, o - 1], ag_r.at[c, o - 1], dev(seg, lax.rem(z + o, ZS), x)).start()

    for c in range(CH):
        for o in order[::-1]:
            p_src = piece(c, lax.rem(z + ZS - o, ZS))

            @pl.when(p_src < PC)
            def _():
                arrived(zr.at[c, o - 1], ag_r.at[c, o - 1])

        quarter = grad.at[:, c, pl.ds(3 * x, 3)]
        for o in (2, 1, 3):
            remote(quarter, quarter, xg_s.at[c, o - 1], xg_r.at[c, o - 1], dev(seg, z, lax.rem(x + o, XS))).start()

    for j in range(MB):
        arrived(stash.at[j], ss_r.at[j])
    for j in range(WIN):
        @pl.when(k * WIN + j != z)
        def _():
            arrived(xout.at[:, pl.ds(j * 64, 64)], ss_s.at[j])

    regroup_sent(cot, ct_s)

    @pl.when(jnp.logical_not(last))
    def _():
        for h in range(2):
            arrived(xout.at[:, pl.ds(h * 128, 128)], rl_s.at[h])
        for kk in range(WIN):
            arrived(st_out, st_s.at[kk])
        edges_sent(xout)

    @pl.when(first)
    def _():
        regroup_sent(clips, cg_s)
        for i in range(MB):
            for kk in range(WIN):
                posted(st_clip.at[i], sc_s.at[i * WIN + kk], i * WIN + kk)

            @pl.when(goes_up)
            def _():
                posted(low.at[i], sc_s.at[16 + i], i * WIN + m - 1)

            @pl.when(goes_down)
            def _():
                posted(high.at[i], sc_s.at[16 + i], i * WIN + m + 1)

    for c in range(CH):
        for o in range(1, XS):
            arrived(xr.at[c, o - 1], xs_s.at[c, o - 1])
        for o in range(1, ZS):
            @pl.when(piece(c, lax.rem(z + o, ZS)) < PC)
            def _():
                arrived(zr.at[c, o - 1], zs_s.at[c, o - 1])

        @pl.when(piece(c, z) < PC)
        def _():
            for o in range(1, ZS):
                arrived(zr.at[c, o - 1], ag_s.at[c, o - 1])

    for c in range(CH):
        for o in range(1, XS):
            arrived(grad.at[:, c, pl.ds(3 * lax.rem(x + XS - o, XS), 3)], xg_r.at[c, o - 1])
            arrived(xr.at[c, o - 1], xg_s.at[c, o - 1])


def per_device(clips, lengths, conv_weight, norm_gain, norm_shift, conv_bias, cotangent):
    vmem, anyspace = pltpu.VMEM, pl.ANY
    dma = pltpu.SemaphoreType.DMA
    stash, grad = pl.pallas_call(
        kernel,
        out_shape=(
            jax.ShapeDtypeStruct((MB, FR, 64, C), BF16),
            jax.ShapeDtypeStruct((3, CH, 12, PR, C), BF16),
        ),
        in_specs=[pl.BlockSpec(memory_space=anyspace)] * 7,
        out_specs=(pl.BlockSpec(memory_space=vmem), pl.BlockSpec(memory_space=vmem)),
        scratch_shapes=[
            vmem((MB, FR, 64, C), BF16),
            pltpu.SMEM((MB, 1), jnp.int32),
            vmem((1, C), F32), vmem((1, C), F32), vmem((1, C), F32),
            vmem((FR, CELLS, C), BF16),
            vmem((FR, CELLS, C), BF16),
            vmem((2, FR, 16, C), BF16),
            vmem((9 * C, 3 * C), BF16),
            vmem((3, ROWS + 2, 2, 16, C), BF16),
            vmem((FR, CELLS, C), BF16),
            vmem((ROWS, 2, 16, 3 * C), BF16),
            vmem((CH, XS, PC, PR, C), BF16),
            vmem((CH, XS - 1, PC, PR, C), BF16),
            vmem((CH, PC, PR, C), BF16),
            vmem((CH, ZS - 1, PR, C), BF16),
            vmem((2, 8, C), F32),
            vmem((ZS, 2, 8, C), F32),
            vmem((MB, 2, 8, C), F32),
            vmem((2, 8, C), F32),
            pltpu.SemaphoreType.REGULAR,
            dma((5,)),
            dma((3,)),
            dma((4,)), dma((4,)), dma((4,)), dma((4,)), dma((4,)), dma((4,)),
            dma((2,)), dma((2,)), dma((2,)), dma((2,)), dma((4,)), dma((4,)),
            dma((20,)), dma((16,)),
            dma((3, 3)), dma((3, 3)), dma((3, 15)), dma((3, 15)), dma((3, 15)), dma((3, 15)), dma((3, 3)), dma((3, 3)),
        ],
        compiler_params=pltpu.CompilerParams(
            collective_id=0, has_side_effects=True, vmem_limit_bytes=63 * 2**20),
        cost_estimate=pl.CostEstimate(flops=2 * 10**9, bytes_accessed=4 * 10**6, transcendentals=10**6),
    )(
        clips.reshape(MB, FR, 64, C), lengths, conv_weight[0], norm_gain, norm_shift, conv_bias,
        cotangent.reshape(MB, FR, 64, C))
    grads = grad.reshape(27 * C, C).astype(F32)
    return stash.reshape(1, MB, 1, FR, 8, 8, C), grads[None]


def solution(mesh):
    in_specs = (
        P(None, "dp", None, "rows", None, None),
        P(None, "dp"),
        P("segment", None, None),
        P("segment", None),
        P("segment", None),
        P("segment", None),
        P("segment", None, "dp", None, "rows", None, None),
    )
    out_specs = (P("segment", None, "dp", None, "rows", None, None), P("segment", None, None))
    return jax.shard_map(per_device, mesh=mesh, in_specs=in_specs, out_specs=out_specs, check_vma=False)
```

time: 151 us -> 136 us (0.901)
  Pallas kernels: 142 us -> 130 us
  local copies, waits for them, and re-layouts: 6.53 us -> 2.02 us
    pallas_call x1, Pallas kernels: 142 us -> 130 us  [per_device(): pl.pallas_call(kernel, out_shape=(jax.ShapeDtypeStruct((MB, FR, 64, C), B...]
    unnamed x14 -> x4, local copies, waits for them, and re-layouts: 6.47 us -> 2.02 us
where the time goes in v2:
time: 136 us; the launch traced here: 135 us
  Pallas kernels  130 us (96%)
  other arithmetic  2.53 us (2%)
  local copies, waits for them, and re-layouts  2.02 us (1%)
    pallas_call x1, Pallas kernels, per_device(): pl.pallas_call(kernel, out_shape=(jax.ShapeDtypeStruct((MB, FR, 64, C), B...  130 us

profile of v2, /device:TPU:25, one launch (start us, length us, event | category | flops | bytes accessed | tf_op | source)
XLA Modules:
  0.0 135.3 jit_solution(12326471627072411143)
XLA Ops:
  0.6 1.3 copy.9.lengths_any
  1.9 130.1 %shard_map.86 = (bf16[4,4,64,128]{3,2,1,0:T(8,128)(2,1)}, bf16[3,3,12,32,128]{4,3,2,1,0:T(8,128)(2,1)}) custom-call(bf16[4,4,64,128]{3,2,1,0:T(8,128)(2,1)} %bitcast.11, s32[4,1]{1,0:T(4,128)} %copy.9.lengths_any, bf16[3456,128]{1,0:T(8,128)(2,1)} %bitcast.10, f32[1,128]{1,0:T(1,128)} %gain_any.1, f32[1,128]{1,0:T(1,128)} %shift_any.1, f32[1,128]{1,0:T(1,128)} %bias_any.1, ...), custom_call_target="tpu_custom_call" | custom-call | flops 2000000000 | bytes 4000000 | tf_op jit(solution)/shard_map/pallas_call | solution.py:458
  132.1 0.0 copy-start
  132.1 2.5 %convert.1 = f32[1,3456,128]{2,1,0:T(8,128)} convert(bf16[1,3456,128]{2,1,0:T(8,128)(2,1)} %bitcast.8) | non-fusion elementwise | flops 442368 | bytes 2654208 | tf_op jit(solution)/shard_map/convert_element_type | solution.py:499
  134.6 0.0 copy-done
  134.6 0.7 copy.12
Async XLA Ops:
  132.1 2.5 %copy-start = (bf16[4,4,64,128]{3,2,1,0:T(8,128)(2,1)S(1)}, bf16[4,4,64,128]{3,2,1,0:T(8,128)(2,1)}, u32[]{:S(2)}) copy-start(bf16[4,4,64,128]{3,2,1,0:T(8,128)(2,1)} %get-tuple-element.4) | copy-start | bytes 786436

commit v3 on v2

--- a/solution.py
+++ b/solution.py
@@ -103,7 +103,7 @@
             def _():
                 arrived(src.at[i], ssem.at[i])
 
-    length = lengths[m, 0]
+    length = lengths[m]
     mask = [jnp.where(f < length, 1.0, 0.0).astype(F32) for f in range(FR)]
     n_dev = (length * CELLS).astype(F32)
 
@@ -188,7 +188,7 @@
                 post(high.at[i], halo.at[0], sc_s.at[16 + i], hl_r.at[0], i * WIN + m + 1)
 
         for i in range(MB):
-            here = lengths[i, 0]
+            here = lengths[i]
             masks = [jnp.where(f < here, 1.0, 0.0).astype(F32) for f in range(FR)]
             st_clip[i, 0], st_clip[i, 1] = stats_of(clips.at[i], 8, masks, (here * 64).astype(F32))
             for kk in range(WIN):
@@ -326,11 +326,24 @@
         for kk in range(WIN):
             remote(st_out, st_in.at[k], st_s.at[kk], st_r.at[k], dev(nxt, m * WIN + kk, x)).start()
 
+    def send_stash():
+        for j in range(WIN):
+            to = k * WIN + j
+            src = xout.at[:, pl.ds(j * 64, 64)]
+
+            @pl.when(to != z)
+            def _():
+                remote(src, stash.at[m], ss_s.at[j], ss_r.at[m], dev(seg, to, x)).start()
+
+            @pl.when(to == z)
+            def _():
+                pltpu.make_async_copy(src, stash.at[m], ss_r.at[m]).start()
+
     @pl.when(jnp.logical_and(seg % 2 == 1, jnp.logical_not(last)))
     def _():
         pl.semaphore_signal(go, inc=1, device_id=dev(seg - 1, z, x), device_id_type=MESH)
 
-    @pl.when(jnp.logical_and(seg % 2 == 0, seg < SEGS - 2))
+    @pl.when(first)
     def _():
         pl.semaphore_wait(go, 1)
 
@@ -338,17 +351,9 @@
     def _():
         regroup(cot, cotz, ct_s, ct_r)
 
-    for j in range(WIN):
-        to = k * WIN + j
-        src = xout.at[:, pl.ds(j * 64, 64)]
-
-        @pl.when(to != z)
-        def _():
-            remote(src, stash.at[m], ss_s.at[j], ss_r.at[m], dev(seg, to, x)).start()
-
-        @pl.when(to == z)
-        def _():
-            pltpu.make_async_copy(src, stash.at[m], ss_r.at[m]).start()
+    @pl.when(seg == SEGS - 2)
+    def _():
+        send_stash()
 
     @pl.when(jnp.logical_not(last))
     def _():
@@ -358,6 +363,10 @@
 
     def piece(c, zz):
         return lax.rem(zz + 2 * ZS - PC * c, ZS)
+
+    @pl.when(jnp.logical_and(seg % 2 == 0, jnp.logical_and(seg > 0, seg < SEGS - 2)))
+    def _():
+        pl.semaphore_wait(go, 1)
 
     for c in range(CH):
         for o in (1, 3, 2):
@@ -374,6 +383,10 @@
             @pl.when(p_to < PC)
             def _():
                 remote(zs.at[c, p_to], zr.at[c, o - 1], zs_s.at[c, o - 1], zs_r.at[c, o - 1], dev(seg, to, x)).start()
+
+    @pl.when(seg != SEGS - 2)
+    def _():
+        send_stash()
 
     for c in range(CH):
         mine = piece(c, z)
@@ -465,7 +478,7 @@
         out_specs=(pl.BlockSpec(memory_space=vmem), pl.BlockSpec(memory_space=vmem)),
         scratch_shapes=[
             vmem((MB, FR, 64, C), BF16),
-            pltpu.SMEM((MB, 1), jnp.int32),
+            pltpu.SMEM((MB,), jnp.int32),
             vmem((1, C), F32), vmem((1, C), F32), vmem((1, C), F32),
             vmem((FR, CELLS, C), BF16),
             vmem((FR, CELLS, C), BF16),
@@ -494,7 +507,7 @@
             collective_id=0, has_side_effects=True, vmem_limit_bytes=63 * 2**20),
         cost_estimate=pl.CostEstimate(flops=2 * 10**9, bytes_accessed=4 * 10**6, transcendentals=10**6),
     )(
-        clips.reshape(MB, FR, 64, C), lengths, conv_weight[0], norm_gain, norm_shift, conv_bias,
+        clips.reshape(MB, FR, 64, C), lengths.reshape(MB), conv_weight[0], norm_gain, norm_shift, conv_bias,
         cotangent.reshape(MB, FR, 64, C))
     grads = grad.reshape(27 * C, C).astype(F32)
     return stash.reshape(1, MB, 1, FR, 8, 8, C), grads[None]

time: 136 us -> 127 us (0.934)
  the two profiles are of different devices: /device:TPU:25 before, /device:TPU:57 now
where the time goes in v3:
time: 127 us
  Pallas kernels  123 us (97%)
  other arithmetic  2.53 us (2%)
    pallas_call x1, Pallas kernels, per_device(): pl.pallas_call(kernel, out_shape=(jax.ShapeDtypeStruct((MB, FR, 64, C), B...  123 us

profile of v3, /device:TPU:57, one launch (start us, length us, event | category | flops | bytes accessed | tf_op | source)
XLA Modules:
  0.0 126.9 jit_solution(9221236535007088902)
XLA Ops:
  0.6 123.0 %shard_map.86 = (bf16[4,4,64,128]{3,2,1,0:T(8,128)(2,1)}, bf16[3,3,12,32,128]{4,3,2,1,0:T(8,128)(2,1)}) custom-call(bf16[4,4,64,128]{3,2,1,0:T(8,128)(2,1)} %bitcast.12, s32[4]{0:T(128)} %bitcast.14, bf16[3456,128]{1,0:T(8,128)(2,1)} %bitcast.11, f32[1,128]{1,0:T(1,128)} %gain_any.1, f32[1,128]{1,0:T(1,128)} %shift_any.1, f32[1,128]{1,0:T(1,128)} %bias_any.1, ...), custom_call_target="tpu_custom_call" | custom-call | flops 2000000000 | bytes 4000000 | tf_op jit(solution)/shard_map/pallas_call | solution.py:471
  123.7 0.0 copy-start
  123.7 2.5 %convert.1 = f32[1,3456,128]{2,1,0:T(8,128)} convert(bf16[1,3456,128]{2,1,0:T(8,128)(2,1)} %bitcast.9) | non-fusion elementwise | flops 442368 | bytes 2654208 | tf_op jit(solution)/shard_map/convert_element_type | solution.py:512
  126.2 0.0 copy-done
  126.2 0.7 copy.11
Async XLA Ops:
  123.7 2.5 %copy-start = (bf16[4,4,64,128]{3,2,1,0:T(8,128)(2,1)S(1)}, bf16[4,4,64,128]{3,2,1,0:T(8,128)(2,1)}, u32[]{:S(2)}) copy-start(bf16[4,4,64,128]{3,2,1,0:T(8,128)(2,1)} %get-tuple-element.4) | copy-start | bytes 786436

commit v4 on v3

--- a/solution.py
+++ b/solution.py
@@ -384,7 +384,7 @@
             def _():
                 remote(zs.at[c, p_to], zr.at[c, o - 1], zs_s.at[c, o - 1], zs_r.at[c, o - 1], dev(seg, to, x)).start()
 
-    @pl.when(seg != SEGS - 2)
+    @pl.when(jnp.logical_and(seg != SEGS - 2, jnp.logical_not(last)))
     def _():
         send_stash()
 
@@ -401,6 +401,10 @@
             kept[...] = v.astype(BF16)
             for o in order:
                 remote(kept, kept, ag_s.at[c, o - 1], ag_r.at[c, o - 1], dev(seg, lax.rem(z + o, ZS), x)).start()
+
+    @pl.when(last)
+    def _():
+        send_stash()
 
     for c in range(CH):
         for o in order[::-1]:

time: 127 us -> 122 us (0.961)
  the two profiles are of different devices: /device:TPU:57 before, /device:TPU:49 now
where the time goes in v4:
time: 122 us
  Pallas kernels  118 us (97%)
  other arithmetic  2.53 us (2%)
    pallas_call x1, Pallas kernels, per_device(): pl.pallas_call(kernel, out_shape=(jax.ShapeDtypeStruct((MB, FR, 64, C), B...  118 us
    convert_element_type x1, other arithmetic, per_device(): grads = grad.reshape(27 * C, C).astype(F32)  2.53 us

profile of v4, /device:TPU:49, one launch (start us, length us, event | category | flops | bytes accessed | tf_op | source)
XLA Modules:
  0.0 121.7 jit_solution(1671606309898838389)
XLA Ops:
  0.6 117.8 %shard_map.86 = (bf16[4,4,64,128]{3,2,1,0:T(8,128)(2,1)}, bf16[3,3,12,32,128]{4,3,2,1,0:T(8,128)(2,1)}) custom-call(bf16[4,4,64,128]{3,2,1,0:T(8,128)(2,1)} %bitcast.12, s32[4]{0:T(128)} %bitcast.14, bf16[3456,128]{1,0:T(8,128)(2,1)} %bitcast.11, f32[1,128]{1,0:T(1,128)} %gain_any.1, f32[1,128]{1,0:T(1,128)} %shift_any.1, f32[1,128]{1,0:T(1,128)} %bias_any.1, ...), custom_call_target="tpu_custom_call" | custom-call | flops 2000000000 | bytes 4000000 | tf_op jit(solution)/shard_map/pallas_call | solution.py:475
  118.4 0.0 copy-start
  118.4 2.5 %convert.1 = f32[1,3456,128]{2,1,0:T(8,128)} convert(bf16[1,3456,128]{2,1,0:T(8,128)(2,1)} %bitcast.9) | non-fusion elementwise | flops 442368 | bytes 2654208 | tf_op jit(solution)/shard_map/convert_element_type | solution.py:516
  121.0 0.0 copy-done
  121.0 0.7 copy.11
Async XLA Ops:
  118.4 2.5 %copy-start = (bf16[4,4,64,128]{3,2,1,0:T(8,128)(2,1)S(1)}, bf16[4,4,64,128]{3,2,1,0:T(8,128)(2,1)}, u32[]{:S(2)}) copy-start(bf16[4,4,64,128]{3,2,1,0:T(8,128)(2,1)} %get-tuple-element.4) | copy-start | bytes 786436

commit v5 on v4

--- a/solution.py
+++ b/solution.py
@@ -203,60 +203,7 @@
     def _():
         regroup(cot, cotz, ct_s, ct_r)
 
-    @pl.when(seg > 0)
-    def _():
-        for h in range(2):
-            arrived(xin.at[:, pl.ds(h * 128, 128)], rl_r.at[h])
-        for kk in range(WIN):
-            arrived(st_in.at[kk], st_r.at[kk])
-        combine([(st_in[kk, 0], st_in[kk, 1]) for kk in range(WIN)], n_dev)
-
-    @pl.when(k > 0)
-    def _():
-        arrived(halo.at[0], hl_r.at[0])
-
-    @pl.when(k < WIN - 1)
-    def _():
-        arrived(halo.at[1], hl_r.at[1])
-
-    mean = norm[0]
-    scale = norm[1] * gain[...]
-    offset = jnp.broadcast_to(shift[...], (8, C))
-    col = lax.broadcasted_iota(jnp.int32, (1, 8, C), 1)
-
-    def act(v):
-        v = (v - mean[None]) * scale[None] + offset[None]
-        return v / (1.0 + jnp.exp(-v))
-
-    def put(row, n, per_frame):
-        for fp in range(2):
-            pair = [per_frame[2 * fp], per_frame[2 * fp + 1]]
-            for d in range(3):
-                if d == 0:
-                    out = [jnp.where(col == 0, 0.0, pltpu.roll(h.reshape(n * 8, C), 1, 0).reshape(n, 8, C)) for h in pair]
-                elif d == 2:
-                    out = [jnp.where(col == 7, 0.0, pltpu.roll(h.reshape(n * 8, C), n * 8 - 1, 0).reshape(n, 8, C)) for h in pair]
-                else:
-                    out = pair
-                hs[d, pl.ds(row, n), fp] = jnp.concatenate(out, axis=1).astype(BF16)
-
-    top_here, bottom_here = k > 0, k < WIN - 1
-    put(0, 1, [jnp.where(top_here, act(halo[0, f, 8:16].astype(F32).reshape(1, 8, C)), 0.0) for f in range(FR)])
-    put(ROWS + 1, 1, [jnp.where(bottom_here, act(halo[1, f, 0:8].astype(F32).reshape(1, 8, C)), 0.0) for f in range(FR)])
-
-    def norm_step(j, c):
-        put(8 * j + 1, 8, [
-            act(xin[f, pl.ds(pl.multiple_of(j * 64, 64), 64)].astype(F32).reshape(8, 8, C)) for f in range(FR)])
-        return c
-
-    lax.fori_loop(0, ROWS // 8, norm_step, 0)
-
-    for cp in w_copies:
-        cp.wait()
-
-    factor = 1.0 / math.sqrt(MB * XS * FR * 128 * 8)
-
-    def gradient():
+    def prepare():
         regroup_recv(cotz, ct_r)
 
         def rhs_step(j, c):
@@ -275,6 +222,69 @@
             return c
 
         lax.fori_loop(0, ROWS // 8, rhs_step, 0)
+
+    @pl.when(seg > 1)
+    def _():
+        prepare()
+
+    @pl.when(seg > 0)
+    def _():
+        for h in range(2):
+            arrived(xin.at[:, pl.ds(h * 128, 128)], rl_r.at[h])
+        for kk in range(WIN):
+            arrived(st_in.at[kk], st_r.at[kk])
+        combine([(st_in[kk, 0], st_in[kk, 1]) for kk in range(WIN)], n_dev)
+
+    @pl.when(k > 0)
+    def _():
+        arrived(halo.at[0], hl_r.at[0])
+
+    @pl.when(k < WIN - 1)
+    def _():
+        arrived(halo.at[1], hl_r.at[1])
+
+    mean = norm[0]
+    scale = norm[1] * gain[...]
+    offset = jnp.broadcast_to(shift[...], (8, C))
+    col = lax.broadcasted_iota(jnp.int32, (1, 8, C), 1)
+
+    def act(v):
+        v = (v - mean[None]) * scale[None] + offset[None]
+        return v / (1.0 + jnp.exp(-v))
+
+    def put(row, n, per_frame):
+        for fp in range(2):
+            pair = [per_frame[2 * fp], per_frame[2 * fp + 1]]
+            for d in range(3):
+                if d == 0:
+                    out = [jnp.where(col == 0, 0.0, pltpu.roll(h.reshape(n * 8, C), 1, 0).reshape(n, 8, C)) for h in pair]
+                elif d == 2:
+                    out = [jnp.where(col == 7, 0.0, pltpu.roll(h.reshape(n * 8, C), n * 8 - 1, 0).reshape(n, 8, C)) for h in pair]
+                else:
+                    out = pair
+                hs[d, pl.ds(row, n), fp] = jnp.concatenate(out, axis=1).astype(BF16)
+
+    top_here, bottom_here = k > 0, k < WIN - 1
+    put(0, 1, [jnp.where(top_here, act(halo[0, f, 8:16].astype(F32).reshape(1, 8, C)), 0.0) for f in range(FR)])
+    put(ROWS + 1, 1, [jnp.where(bottom_here, act(halo[1, f, 0:8].astype(F32).reshape(1, 8, C)), 0.0) for f in range(FR)])
+
+    def norm_step(j, c):
+        put(8 * j + 1, 8, [
+            act(xin[f, pl.ds(pl.multiple_of(j * 64, 64), 64)].astype(F32).reshape(8, 8, C)) for f in range(FR)])
+        return c
+
+    lax.fori_loop(0, ROWS // 8, norm_step, 0)
+
+    for cp in w_copies:
+        cp.wait()
+
+    factor = 1.0 / math.sqrt(MB * XS * FR * 128 * 8)
+
+    def gradient():
+        @pl.when(seg <= 1)
+        def _():
+            prepare()
+
         for b in range(CH):
             lhs = jnp.concatenate([hs[d, b:b + ROWS].reshape(ROWS * 32, C) for d in range(3)], axis=1)
             acc = lax.dot_general(

time: 122 us -> 122 us (level)
  the two profiles are of different devices: /device:TPU:49 before, /device:TPU:25 now
where the time goes in v5:
time: 122 us; the launch traced here: 121 us
  Pallas kernels  117 us (96%)
  other arithmetic  2.53 us (2%)
    pallas_call x1, Pallas kernels, per_device(): pl.pallas_call(kernel, out_shape=(jax.ShapeDtypeStruct((MB, FR, 64, C), B...  117 us
    convert_element_type x1, other arithmetic, per_device(): grads = grad.reshape(27 * C, C).astype(F32)  2.53 us

profile of v5, /device:TPU:25, one launch (start us, length us, event | category | flops | bytes accessed | tf_op | source)
XLA Modules:
  0.0 120.6 jit_solution(6561047901503066796)
XLA Ops:
  0.6 116.7 %shard_map.86 = (bf16[4,4,64,128]{3,2,1,0:T(8,128)(2,1)}, bf16[3,3,12,32,128]{4,3,2,1,0:T(8,128)(2,1)}) custom-call(bf16[4,4,64,128]{3,2,1,0:T(8,128)(2,1)} %bitcast.12, s32[4]{0:T(128)} %bitcast.14, bf16[3456,128]{1,0:T(8,128)(2,1)} %bitcast.11, f32[1,128]{1,0:T(1,128)} %gain_any.1, f32[1,128]{1,0:T(1,128)} %shift_any.1, f32[1,128]{1,0:T(1,128)} %bias_any.1, ...), custom_call_target="tpu_custom_call" | custom-call | flops 2000000000 | bytes 4000000 | tf_op jit(solution)/shard_map/pallas_call | solution.py:485
  117.3 0.0 copy-start
  117.3 2.5 %convert.1 = f32[1,3456,128]{2,1,0:T(8,128)} convert(bf16[1,3456,128]{2,1,0:T(8,128)(2,1)} %bitcast.9) | non-fusion elementwise | flops 442368 | bytes 2654208 | tf_op jit(solution)/shard_map/convert_element_type | solution.py:526
  119.9 0.0 copy-done
  119.9 0.7 copy.11
Async XLA Ops:
  117.3 2.5 %copy-start = (bf16[4,4,64,128]{3,2,1,0:T(8,128)(2,1)S(1)}, bf16[4,4,64,128]{3,2,1,0:T(8,128)(2,1)}, u32[]{:S(2)}) copy-start(bf16[4,4,64,128]{3,2,1,0:T(8,128)(2,1)} %get-tuple-element.4) | copy-start | bytes 786436
